TPU v7x, 128 devices: a whole 4x4x4 slice. The times are simulated.
128 devices in a mesh: ctx: 16 (over y, z_lo, core), fsdp: 8 (over x, z_hi).
Axes of the slice: x: 4, y: 4, z: 4 (z_hi: 2, z_lo: 2; z = z_hi * 2 + z_lo), core: 2. Of those that a mesh axis runs over, the one named last changes fastest.
Arguments:
- tokens: bfloat16 [8, 2048, 2048], P('fsdp', 'ctx'), may hold values from -6 to 6
- cotangent: bfloat16 [8, 2048, 2048], P('fsdp', 'ctx'), may hold values from -6 to 6
- block_order: int32 [32], replicated, may hold values from 0 to 31, as said below
- positions: int32 [8, 2048], P('fsdp', 'ctx'), may hold values from 0 to 4094, as said below
- ln_gain: bfloat16 [2048], P('fsdp'), may hold values from 0.5 to 1.5
- ln_bias: bfloat16 [2048], P('fsdp'), may hold values from -4 to 4
- w_qkv: bfloat16 [2048, 6144], P('fsdp'), may hold values from -0.1875 to 0.1875
- b_qkv: bfloat16 [6144], P('fsdp'), may hold values from -4 to 4
- w_dense: bfloat16 [2048, 2048], P('fsdp'), may hold values from -1 to 1
- b_dense: bfloat16 [2048], P('fsdp'), may hold values from -4 to 4
- w_fc1: bfloat16 [2048, 8192], P('fsdp'), may hold values from -0.125 to 0.125
- b_fc1: bfloat16 [8192], P('fsdp'), may hold values from -6 to 6
- w_fc2: bfloat16 [8192, 2048], P('fsdp'), may hold values from -0.0625 to 0.0625
- b_fc2: bfloat16 [2048], P('fsdp'), may hold values from -4 to 4
Outputs:
- output: bfloat16 [8, 2048, 2048], P('fsdp', 'ctx')
- input_grad: float32 [8, 2048, 2048], P('fsdp', 'ctx')
- grad_ln_gain: float32 [2048], P('fsdp')
- grad_ln_bias: float32 [2048], P('fsdp')
- grad_w_qkv: float32 [2048, 6144], P('fsdp')
- grad_b_qkv: float32 [6144], P('fsdp')
- grad_w_dense: float32 [2048, 2048], P('fsdp')
- grad_b_dense: float32 [2048], P('fsdp')
- grad_w_fc1: float32 [2048, 8192], P('fsdp')
- grad_b_fc1: float32 [8192], P('fsdp')
- grad_w_fc2: float32 [8192, 2048], P('fsdp')
- grad_b_fc2: float32 [2048], P('fsdp')
Inputs may be any that keep to these rules, and one draw needn't show every extreme that they name: `block_order`: a permutation of the block numbers; the two stored blocks of each ctx device (entries 2c and 2c + 1) add up to 31, in either order. Taken in the initial token order of each sequence, positions start at 0, rise by 1 to 3 from token to token, and the last token's position is 4094.
All inputs are finite; a program needn't handle non-finite values.
Results may differ from a plain program's by a relative error of at most 0.024.
Values may be sent and summed in bfloat16 or wider, within the bound.
A program may use at most 512 MiB of HBM per device.

v0:
```python
import jax
import jax.numpy as jnp
from jax import lax
from jax.sharding import PartitionSpec as P

HEADS = 32
HEAD_DIM = 64
ROTARY = 32


NORM_EPS = 1e-05
ROPE_BASE = 10000.0
GELU_COEF = 0.7978845608028654


def gelu_tanh(values):
    return (
        0.5 * values * (1.0 + jnp.tanh(GELU_COEF * (values + 0.044715 * values * values * values)))
    )


def angles(positions):
    frequency = ROPE_BASE ** (-(jnp.arange(ROTARY // 2, dtype=jnp.float32) * (2.0 / ROTARY)))
    turned = positions.astype(jnp.float32)[..., None] * frequency
    return (jnp.cos(turned)[..., None, :], jnp.sin(turned)[..., None, :])


def rotate(headed, cosine, sines):
    half_rot = cosine.shape[-1]
    first_half = headed[..., :half_rot]
    second_half = headed[..., half_rot : 2 * half_rot]
    rest_dims = headed[..., 2 * half_rot :]
    return jnp.concatenate(
        [
            first_half * cosine - second_half * sines,
            second_half * cosine + first_half * sines,
            rest_dims,
        ],
        axis=-1,
    )


def layer_norm(values_in, gain_full, shift_full):
    centre_mean = jnp.mean(values_in, axis=-1, keepdims=True)
    centered = values_in - centre_mean
    variance = jnp.mean(centered * centered, axis=-1, keepdims=True)
    return centered * lax.rsqrt(variance + NORM_EPS) * gain_full + shift_full


def reduce_rows(term_fn, own_rows):
    shard_part = lax.psum_scatter(
        term_fn(jnp.int32(0), own_rows * lax.axis_size("fsdp")).astype(jnp.bfloat16),
        "fsdp",
        scatter_dimension=0,
        tiled=True,
    )
    return lax.psum(shard_part, "ctx").astype(jnp.float32)


def on_device(
    tokens,
    cotangent,
    block_order,
    positions,
    ln_gain,
    ln_bias,
    w_qkv,
    b_qkv,
    w_dense,
    b_dense,
    w_fc1,
    b_fc1,
    w_fc2,
    b_fc2,
):
    row_count = tokens.shape[1]
    model_width = tokens.shape[2]
    ff_width = w_fc1.shape[1]
    shard_rows = w_dense.shape[0]
    hidden_ratio = ff_width // model_width
    score_scale = HEAD_DIM ** (-0.5)
    head_groups = 4
    group_heads = HEADS // head_groups
    flat_contract = (((1,), (1,)), ((), ()))
    row_contract = (((0,), (0,)), ((), ()))
    inputs_f = tokens.reshape(row_count, model_width).astype(jnp.float32)
    grad_out = cotangent.reshape(row_count, model_width)
    gain, shift, bias_qkv, bias_fc1, bias_dense, bias_fc2 = (
        lax.all_gather(ln_gain, "fsdp", axis=0, tiled=True),
        lax.all_gather(ln_bias, "fsdp", axis=0, tiled=True),
        lax.all_gather(b_qkv, "fsdp", axis=0, tiled=True),
        lax.all_gather(b_fc1, "fsdp", axis=0, tiled=True),
        lax.all_gather(b_dense, "fsdp", axis=0, tiled=True),
        lax.all_gather(b_fc2, "fsdp", axis=0, tiled=True),
    )
    gain_full = gain.astype(jnp.float32)
    shift_full = shift.astype(jnp.float32)
    hidden = layer_norm(inputs_f, gain_full, shift_full).astype(jnp.bfloat16)
    pieces = (
        lax.all_gather(w_qkv, "fsdp", axis=0, tiled=True),
        lax.all_gather(w_fc1, "fsdp", axis=0, tiled=True),
    )
    amount = pieces[0].shape[0]
    projected = jnp.dot(hidden, pieces[0], preferred_element_type=jnp.float32)
    up_value = jnp.dot(hidden, pieces[1], preferred_element_type=jnp.float32)
    projected = projected + bias_qkv.astype(jnp.float32)
    up_value = up_value + bias_fc1.astype(jnp.float32)
    cosine, sines = angles(positions.reshape(row_count))
    head_shape = (row_count, HEADS, HEAD_DIM)
    q_rot = rotate(projected[:, :model_width].reshape(head_shape), cosine, sines).astype(
        jnp.bfloat16
    )
    k_rot = (
        rotate(projected[:, model_width : 2 * model_width].reshape(head_shape), cosine, sines)
        .astype(jnp.bfloat16)
        .reshape(row_count, model_width)
    )
    v_low = projected[:, 2 * model_width :].astype(jnp.bfloat16)
    keys_all, values_all = (
        lax.all_gather(k_rot, "ctx", axis=0, tiled=True),
        lax.all_gather(v_low, "ctx", axis=0, tiled=True),
    )
    key_count = keys_all.shape[0]
    block_rows = row_count // 2
    ctx_place = lax.axis_index("ctx")
    my_blocks = lax.dynamic_slice_in_dim(block_order, 2 * ctx_place, 2, 0)
    offsets = jnp.arange(block_rows, dtype=jnp.int32)
    query_anchor = (my_blocks[:, None] * block_rows + offsets[None, :]).reshape(row_count)
    key_anchor = (block_order[:, None] * block_rows + offsets[None, :]).reshape(key_count)
    allowed = key_anchor[None, :] <= query_anchor[:, None]

    def split_heads(values_in, length):
        return values_in.reshape(length, head_groups, group_heads, HEAD_DIM).transpose(1, 0, 2, 3)

    def join_heads(values_in, length):
        return values_in.transpose(1, 0, 2, 3).reshape(length, model_width)

    def forward_group(parts):
        query_part, key_part, value_part = parts
        scores = (
            jnp.einsum("qhd,khd->hqk", query_part, key_part, preferred_element_type=jnp.float32)
            * score_scale
        )
        masked = jnp.where(allowed[None], scores, -1e30)
        peak = jnp.max(masked, axis=-1, keepdims=True)
        weights = jnp.exp(masked - peak)
        mass = jnp.sum(weights, axis=-1, keepdims=True)
        probs = (weights / mass).astype(jnp.bfloat16)
        mixed_out = jnp.einsum(
            "hqk,khd->qhd", probs, value_part, preferred_element_type=jnp.float32
        )
        return (mixed_out, peak[..., 0] + jnp.log(mass[..., 0]))

    q_groups = split_heads(q_rot, row_count)
    k_groups = split_heads(keys_all, key_count)
    v_groups = split_heads(values_all, key_count)
    mixed_out, logsum = lax.map(forward_group, (q_groups, k_groups, v_groups))
    attended = join_heads(mixed_out, row_count).astype(jnp.bfloat16)
    activated = gelu_tanh(up_value).astype(jnp.bfloat16)
    w_fc2_rows = w_fc2.reshape(shard_rows, hidden_ratio * model_width)
    pieces = (
        lax.all_gather(w_dense, "fsdp", axis=0, tiled=True),
        lax.all_gather(w_fc2_rows, "fsdp", axis=0, tiled=True),
    )
    amount = pieces[0].shape[0]
    widened = pieces[1].reshape(amount * hidden_ratio, model_width)
    branches = jnp.dot(attended, pieces[0], preferred_element_type=jnp.float32) + jnp.dot(
        activated, widened, preferred_element_type=jnp.float32
    )
    result = inputs_f + branches + bias_dense.astype(jnp.float32) + bias_fc2.astype(jnp.float32)
    pieces = (
        lax.all_gather(w_dense, "fsdp", axis=0, tiled=True),
        lax.all_gather(w_fc2_rows, "fsdp", axis=0, tiled=True),
    )
    amount = pieces[0].shape[0]
    widened = pieces[1].reshape(amount * hidden_ratio, model_width)
    attn_part = lax.dot_general(
        grad_out, pieces[0], flat_contract, preferred_element_type=jnp.float32
    )
    act_part = lax.dot_general(grad_out, widened, flat_contract, preferred_element_type=jnp.float32)
    d_attended = attn_part
    d_attended = d_attended.astype(jnp.bfloat16)
    d_up = jax.vjp(gelu_tanh, up_value)[1](act_part)[0].astype(jnp.bfloat16)

    def backward_group(parts):
        query_part, key_part, value_part, grad_part, logsum_part = parts
        scores = (
            jnp.einsum("qhd,khd->hqk", query_part, key_part, preferred_element_type=jnp.float32)
            * score_scale
        )
        probs = jnp.where(allowed[None], jnp.exp(scores - logsum_part[..., None]), 0.0)
        d_probs = jnp.einsum(
            "qhd,khd->hqk", grad_part, value_part, preferred_element_type=jnp.float32
        )
        centre_term = jnp.sum(probs * d_probs, axis=-1, keepdims=True)
        d_scores = (probs * (d_probs - centre_term)).astype(jnp.bfloat16)
        d_query = (
            jnp.einsum("hqk,khd->qhd", d_scores, key_part, preferred_element_type=jnp.float32)
            * score_scale
        )
        d_key = (
            jnp.einsum("hqk,qhd->khd", d_scores, query_part, preferred_element_type=jnp.float32)
            * score_scale
        )
        d_value = jnp.einsum(
            "hqk,qhd->khd",
            probs.astype(jnp.bfloat16),
            grad_part,
            preferred_element_type=jnp.float32,
        )
        return (d_query, d_key, d_value)

    d_groups = split_heads(d_attended, row_count)
    d_query, d_key_part, d_value_part = lax.map(
        backward_group, (q_groups, k_groups, v_groups, d_groups, logsum)
    )
    d_keys, d_values = (
        lax.psum_scatter(
            join_heads(d_key_part, key_count).astype(jnp.bfloat16),
            "ctx",
            scatter_dimension=0,
            tiled=True,
        ).astype(jnp.float32),
        lax.psum_scatter(
            join_heads(d_value_part, key_count).astype(jnp.bfloat16),
            "ctx",
            scatter_dimension=0,
            tiled=True,
        ).astype(jnp.float32),
    )
    d_query_flat = rotate(
        join_heads(d_query, row_count).reshape(head_shape), cosine, -sines
    ).reshape(row_count, model_width)
    d_key_flat = rotate(d_keys.reshape(head_shape), cosine, -sines).reshape(row_count, model_width)
    d_projected = jnp.concatenate([d_query_flat, d_key_flat, d_values], axis=1).astype(jnp.bfloat16)
    pieces = (
        lax.all_gather(w_qkv, "fsdp", axis=0, tiled=True),
        lax.all_gather(w_fc1, "fsdp", axis=0, tiled=True),
    )
    grad_part = lax.dot_general(
        d_projected, pieces[0], flat_contract, preferred_element_type=jnp.float32
    )
    grad_part = grad_part + lax.dot_general(
        d_up, pieces[1], flat_contract, preferred_element_type=jnp.float32
    )
    norm_pullback = jax.vjp(layer_norm, inputs_f, gain_full, shift_full)[1]
    d_inputs, d_gain, d_shift = norm_pullback(grad_part)
    input_grad = grad_out.astype(jnp.float32) + d_inputs
    fsdp_size = lax.axis_size("fsdp")
    own_rows = model_width // fsdp_size

    def qkv_term(offset, amount):
        return lax.dot_general(
            hidden, d_projected, row_contract, preferred_element_type=jnp.float32
        )

    def fc1_term(offset, amount):
        return lax.dot_general(hidden, d_up, row_contract, preferred_element_type=jnp.float32)

    def dense_term(offset, amount):
        return lax.dot_general(attended, grad_out, row_contract, preferred_element_type=jnp.float32)

    def fc2_term(offset, amount):
        lower_rows = lax.dot_general(
            activated, grad_out, row_contract, preferred_element_type=jnp.float32
        )
        return lower_rows.reshape(amount, hidden_ratio * model_width)

    grad_w_qkv = reduce_rows(qkv_term, own_rows)
    grad_w_fc1 = reduce_rows(fc1_term, own_rows)
    grad_w_dense = reduce_rows(dense_term, own_rows)
    grad_w_fc2 = reduce_rows(fc2_term, own_rows).reshape(own_rows * hidden_ratio, model_width)
    column_total = jnp.sum(grad_out.astype(jnp.float32), axis=0)
    small_sums = lax.psum(
        (
            d_gain,
            d_shift,
            jnp.sum(d_projected.astype(jnp.float32), axis=0),
            jnp.sum(d_up.astype(jnp.float32), axis=0),
            column_total,
        ),
        ("ctx", "fsdp"),
    )
    fsdp_place = lax.axis_index("fsdp")

    def own_part(vector):
        length = vector.shape[0] // fsdp_size
        return lax.dynamic_slice_in_dim(vector, fsdp_place * length, length, 0)

    bias_out_grad = own_part(small_sums[4])
    return (
        result.astype(jnp.bfloat16).reshape(1, row_count, model_width),
        input_grad.reshape(1, row_count, model_width),
        own_part(small_sums[0]),
        own_part(small_sums[1]),
        grad_w_qkv,
        own_part(small_sums[2]),
        grad_w_dense,
        bias_out_grad,
        grad_w_fc1,
        own_part(small_sums[3]),
        grad_w_fc2,
        bias_out_grad,
    )


def solution(mesh):
    return jax.shard_map(
        on_device,
        mesh=mesh,
        in_specs=(
            P("fsdp", "ctx", None),
            P("fsdp", "ctx", None),
            P(),
            P("fsdp", "ctx"),
            P("fsdp"),
            P("fsdp"),
            P("fsdp", None),
            P("fsdp"),
            P("fsdp", None),
            P("fsdp"),
            P("fsdp", None),
            P("fsdp"),
            P("fsdp", None),
            P("fsdp"),
        ),
        out_specs=(
            P("fsdp", "ctx", None),
            P("fsdp", "ctx", None),
            P("fsdp"),
            P("fsdp"),
            P("fsdp", None),
            P("fsdp"),
            P("fsdp", None),
            P("fsdp"),
            P("fsdp", None),
            P("fsdp"),
            P("fsdp", None),
            P("fsdp"),
        ),
        check_vma=False,
    )
```

profile of v0, /device:TPU:1, one launch (start us, length us, event | category | flops | bytes accessed | tf_op | source)
XLA Modules:
  0.0 2934.3 jit_solution(3671537237746396248)
XLA Ops:
  8.8 21.2 all-gather.1
  30.1 14.6 all-gather
  44.7 27.6 all-gather.2
  73.4 203.2 %all-gather.12.cloned.1.call-done = bf16[2048,6144]{1,0:T(8,128)(2,1)} async-done(((bf16[256,6144]{1,0:T(8,128)(2,1)}), bf16[2048,6144]{1,0:T(8,128)(2,1)}) %all-gather.12.cloned.1.call-update) | async-done | bytes 25165840 | tf_op jit(solution)/shard_map/all_gather | solution.py:100
  276.6 10.1 convolution_add_fusion.1
  296.2 7.9 reshape.275
  305.3 80.4 %all-gather.18.cloned.1.call-done = bf16[2048,2048]{1,0:T(8,128)(2,1)} async-done(((bf16[256,2048]{1,0:T(8,128)(2,1)}), bf16[2048,2048]{1,0:T(8,128)(2,1)}) %all-gather.18.cloned.1.call-update) | async-done | bytes 8388624 | tf_op jit(solution)/shard_map/all_gather | solution.py:162
  385.6 6.3 convolution_convert_fusion.4
  392.3 46.4 %all-gather.14.cloned.1.call-done = bf16[2048,2048]{1,0:T(8,128)(2,1)} async-done(((bf16[128,2048]{1,0:T(8,128)(2,1)}), bf16[2048,2048]{1,0:T(8,128)(2,1)}) %all-gather.14.cloned.1.call-update) | async-done | bytes 8388624 | tf_op jit(solution)/shard_map/all_gather | solution.py:121
  438.7 12.2 copy.42
  450.9 51.3 %all-gather.16.cloned.1.call-done = bf16[2048,2048]{0,1:T(8,128)(2,1)} async-done(((bf16[128,2048]{0,1:T(8,128)(2,1)}), bf16[2048,2048]{0,1:T(8,128)(2,1)}) %all-gather.16.cloned.1.call-update) | async-done | bytes 8388624 | tf_op jit(solution)/shard_map/all_gather | solution.py:120
  502.2 40.4 %while.30 = (s32[]{:T(128)}, bf16[4,128,8,64]{1,3,2,0:T(8,128)(2,1)S(1)}, f32[4,8,128]{2,1,0:T(8,128)S(1)}, bf16[4,2048,8,64]{1,3,2,0:T(8,128)(2,1)}, bf16[4,128...) while((s32[]{:T(128)}, ...), condition=%wide.region_5.6_spmd.clone.clone, body=%wide.region_2.5_spmd.clone.sunk.clone | while | flops 562297856 | bytes 30845536 | solution.py:157
  518.3 4.5 fusion.153
  543.4 78.3 %while.31 = (s32[]{:T(128)}, f32[4,128,8,64]{1,3,2,0:T(8,128)S(1)}, bf16[4,2048,8,64]{1,3,2,0:T(8,128)(2,1)}, bf16[4,2048,8,64]{1,3,2,0:T(8,128)(2,1)}, bf16[4,2...) while((s32[]{:T(128)}, f32[4,128,8,64]{1,3,2,0:T(8,128)S(1)}, ...), condition=%wide.region_8.9_spmd.clone.clone, body=%wide.region_6.8_spmd.clone.sunk.clone | while | flops 1375009792 | bytes 79472248 | solution.py:214
  550.2 4.8 multiply_reduce_fusion.3
  569.5 4.9 multiply_reduce_fusion.3
  588.9 4.8 multiply_reduce_fusion.3
  608.9 4.9 multiply_reduce_fusion.3
  621.7 12.7 copy.46
  634.5 12.2 copy.48
  647.4 26.6 all_gather.48
  674.0 170.0 %all-gather.20.cloned.1.call-done = bf16[2048,8192]{1,0:T(8,128)(2,1)} async-done(((bf16[256,8192]{1,0:T(8,128)(2,1)}), bf16[2048,8192]{1,0:T(8,128)(2,1)}) %all-gather.20.cloned.1.call-update) | async-done | bytes 33554448 | tf_op jit(solution)/shard_map/all_gather | solution.py:101
  844.0 17.2 convolution_add_fusion
  861.3 17.3 convolution_convert_fusion.1
  878.5 55.2 %convert_element_type.168 = bf16[2048,8192]{1,0:T(8,128)(2,1)} reshape(bf16[8192,2048]{1,0:T(8,128)(2,1)} %convolution_convert_fusion.1) | data formatting | bytes 67108864 | tf_op jit(solution)/shard_map/convert_element_type | solution.py:52
  934.8 5.7 convolution_convert_fusion.3
  940.7 244.0 %all-gather.22.cloned.1.call-done = bf16[2048,8192]{1,0:T(8,128)(2,1)} async-done(((bf16[256,8192]{1,0:T(8,128)(2,1)}), bf16[2048,8192]{1,0:T(8,128)(2,1)}) %all-gather.22.cloned.1.call-update) | async-done | bytes 33554448 | tf_op jit(solution)/shard_map/all_gather | solution.py:163
  1184.7 55.3 %reshape.276 = bf16[8192,2048]{1,0:T(8,128)(2,1)} reshape(bf16[2048,8192]{1,0:T(8,128)(2,1)} %all-gather.22.cloned.1.call-done) | data formatting | bytes 67108864 | tf_op jit(solution)/shard_map/reshape | solution.py:166
  1240.0 19.9 convert_reduce_fusion
  1259.9 14.0 convolution_convert_fusion
  1275.0 7.2 reduce-scatter.19.cloned.1.call-done
  1288.0 94.8 %reduce-scatter.21.cloned.1.call-done = bf16[128,2048]{1,0:T(8,128)(2,1)} async-done(((bf16[2048,2048]{1,0:T(8,128)(2,1)}), bf16[128,2048]{1,0:T(8,128)(2,1)}) %reduce-scatter.21.cloned.1.call-update) | async-done | bytes 524304
  1388.2 13.7 convolution_convert_fusion.2
  1404.6 14.2 fusion.99
  1418.9 18.0 fusion.105
  1440.1 299.5 %reduce-scatter.17.cloned.1.call-done = bf16[256,8192]{1,0:T(8,128)(2,1)} async-done(((bf16[2048,8192]{1,0:T(8,128)(2,1)}), bf16[256,8192]{1,0:T(8,128)(2,1)}) %reduce-scatter.17.cloned.1.call-update) | async-done | bytes 4194320 | tf_op jit(solution)/shard_map/reduce_scatter | solution.py:51
  1739.7 7.9 reshape.285
  1747.6 112.6 %reduce-scatter.13.cloned.1.call-done = bf16[256,2048]{1,0:T(8,128)(2,1)} async-done(((bf16[2048,2048]{1,0:T(8,128)(2,1)}), bf16[256,2048]{1,0:T(8,128)(2,1)}) %reduce-scatter.13.cloned.1.call-update) | async-done | bytes 1048592 | tf_op jit(solution)/shard_map/reduce_scatter | solution.py:51
  1860.1 354.6 %reduce-scatter.15.cloned.1.call-done = bf16[256,8192]{1,0:T(8,128)(2,1)} async-done(((bf16[2048,8192]{1,0:T(8,128)(2,1)}), bf16[256,8192]{1,0:T(8,128)(2,1)}) %reduce-scatter.15.cloned.1.call-update) | async-done | bytes 4194320 | tf_op jit(solution)/shard_map/reduce_scatter | solution.py:51
  2214.7 268.4 %reduce-scatter.11.cloned.1.call-done = bf16[256,6144]{1,0:T(8,128)(2,1)} async-done(((bf16[2048,6144]{1,0:T(8,128)(2,1)}), bf16[256,6144]{1,0:T(8,128)(2,1)}) %reduce-scatter.11.cloned.1.call-update) | async-done | bytes 3145744 | tf_op jit(solution)/shard_map/reduce_scatter | solution.py:51
  2483.8 17.0 all-gather.4
  2500.8 15.6 all-gather.3
  2516.4 4.7 fusion.107
  2521.1 17.9 fusion.76
  2539.0 92.3 %all-reduce.5.cloned.1.call-done = (f32[2048]{0:T(1024)}, f32[2048]{0:T(1024)}, f32[6144]{0:T(1024)}, f32[2048]{0:T(1024)}, f32[8192]{0:T(1024)}) async-done(((f32[2048]{0:T(1024)}, f32[2048]{0:T(1024)}, f32[6144]{0:T(1024)}, f32[2048]{0:T(1024)}, f32[8192]{0:T(1024)}), (f32[2048]{0:T(1024)}, f32[2048]{0:T(1024)}, f32[6144]{0:T(1024)}, f32[2048]{0:T(1024)}, f32[8192]{0:T(1024)})) %all-reduce.5.cloned.1.call-update) | async-done | bytes 81936 | tf_op jit(solution)/shard_map/psum | solution.py:274
  2637.4 274.3 %all-reduce.7.cloned.1.call-done = (bf16[256,6144]{1,0:T(8,128)(2,1)}, bf16[256,2048]{1,0:T(8,128)(2,1)}, bf16[256,8192]{1,0:T(8,128)(2,1)}, bf16[1024,2048]{1,0:T(8,128)(2,1)}) async-done(((bf16[256,6144]{1,0:T(8,128)(2,1)}, bf16[256,2048]{1,0:T(8,128)(2,1)}, bf16[256,8192]{1,0:T(8,128)(2,1)}, bf16[1024,2048]{1,0:T(8,128)(2,1)}), (bf16[256,6144]{1,0:T(8,128)(2,1)}, bf16[256,2048]{1,0:T(8,128)(2,1)}, ...) | async-done | bytes 12582928 | tf_op jit(solution)/shard_map/psum | solution.py:57
  2918.1 4.4 convert_element_type.165
  2922.4 4.4 reshape.286
  (206 shorter events, 142.5 us)
Async XLA Ops:
  7.2 1.6 copy-start.30
  7.2 1.6 copy-start.31
  7.2 1.6 copy-start.27
  7.2 65.2 %copy-start = (bf16[1,128,2048]{2,1,0:T(8,128)(2,1)S(1)}, bf16[1,128,2048]{2,1,0:T(8,128)(2,1)}, u32[]{:S(2)}) copy-start(bf16[1,128,2048]{2,1,0:T(8,128)(2,1)} %param.18) | copy-start | bytes 1572868
  7.2 269.4 %all-gather.12.cloned.1.call-start = ((), (), s32[]{:S(2)}) async-start(), calls=%async_computation.6 | async-start | bytes 28311552 | tf_op jit(solution)/shard_map/all_gather | solution.py:100
  8.0 377.7 %all-gather.18.cloned.1.call-start = ((), (), s32[]{:S(2)}) async-start(), calls=%async_computation.9 | async-start | bytes 9437184 | tf_op jit(solution)/shard_map/all_gather | solution.py:162
  8.7 430.0 %all-gather.14.cloned.1.call-start = ((), (), s32[]{:S(2)}) async-start(), calls=%async_computation.7 | async-start | bytes 8912896 | tf_op jit(solution)/shard_map/all_gather | solution.py:121
  30.1 256.7 %copy-start.14 = (f32[8,1,256]{2,1,0:T(1,128)}, f32[8,1,256]{2,1,0:T(1,128)S(1)}, u32[]{:S(2)}) copy-start(f32[8,1,256]{2,1,0:T(1,128)S(1)} %convert_element_type.170) | copy-start | bytes 24580
  44.7 242.0 %copy-start.12 = (f32[8,1,256]{2,1,0:T(1,128)}, f32[8,1,256]{2,1,0:T(1,128)S(1)}, u32[]{:S(2)}) copy-start(f32[8,1,256]{2,1,0:T(1,128)S(1)} %convert_element_type.169) | copy-start | bytes 24580
  72.6 214.2 %copy-start.18 = (f32[128]{0:T(128)}, f32[128]{0:T(128)S(1)}, u32[]{:S(2)}) copy-start(f32[128]{0:T(128)S(1)} %broadcast_multiply_fusion.1) | copy-start | bytes 1540
  73.4 213.4 %copy-start.20 = (f32[128]{0:T(128)}, f32[128]{0:T(128)S(1)}, u32[]{:S(2)}) copy-start(f32[128]{0:T(128)S(1)} %fusion.98) | copy-start | bytes 1540
  276.6 12.8 copy-start.32
  286.8 1.7 copy-start.2
  289.3 212.9 %all-gather.16.cloned.1.call-start = ((), (), s32[]{:S(2)}) async-start(), calls=%async_computation.8 | async-start | bytes 8912896 | tf_op jit(solution)/shard_map/all_gather | solution.py:120
  290.1 3.3 copy-start.22
  292.2 1.0 copy-start.10
  295.6 548.4 %all-gather.20.cloned.1.call-start = ((), (), s32[]{:S(2)}) async-start(), calls=%async_computation.10 | async-start | bytes 37748736 | tf_op jit(solution)/shard_map/all_gather | solution.py:101
  296.2 888.6 %all-gather.22.cloned.1.call-start = ((), (), s32[]{:S(2)}) async-start(), calls=%async_computation.11 | async-start | bytes 37748736 | tf_op jit(solution)/shard_map/all_gather | solution.py:163
  304.1 0.7 copy-start.33
  304.1 81.5 %copy-start.5 = (bf16[1,128,2048]{2,1,0:T(8,128)(2,1)S(1)}, bf16[1,128,2048]{2,1,0:T(8,128)(2,1)}, u32[]{:S(2)}) copy-start(bf16[1,128,2048]{2,1,0:T(8,128)(2,1)} %param.19) | copy-start | bytes 1572868
  304.1 978.1 %reduce-scatter.19.cloned.1.call-start = ((), (), s32[]{:S(2)}) async-start(), calls=%async_computation.16 | async-start | bytes 8912896
  502.2 40.4 %copy-start.16 = (f32[4,128,8,64]{1,3,2,0:T(8,128)S(1)}, f32[4,128,8,64]{1,3,2,0:T(8,128)}, u32[]{:S(2)}) copy-start(f32[4,128,8,64]{1,3,2,0:T(8,128)} %custom-call.3) | copy-start | bytes 3145732
  542.6 0.8 copy-start.3
  621.7 12.7 copy-start.17
  634.5 748.3 %reduce-scatter.21.cloned.1.call-start = ((), (), s32[]{:S(2)}) async-start(), calls=%async_computation.17 | async-start | bytes 8912896
  646.7 0.7 copy-start.26
  646.7 197.2 %copy-start.1 = (bf16[1,128,2048]{2,1,0:T(8,128)(2,1)S(1)}, bf16[1,128,2048]{2,1,0:T(8,128)(2,1)}, u32[]{:S(2)}) copy-start(bf16[1,128,2048]{2,1,0:T(8,128)(2,1)} %param.18) | copy-start | bytes 1572868
  646.8 197.2 %copy-start.13 = (f32[8,1,256]{2,1,0:T(1,128)S(1)}, f32[8,1,256]{2,1,0:T(1,128)}, u32[]{:S(2)}) copy-start(f32[8,1,256]{2,1,0:T(1,128)} %copy-done.12) | copy-start | bytes 24580
  646.8 197.3 %copy-start.15 = (f32[8,1,256]{2,1,0:T(1,128)S(1)}, f32[8,1,256]{2,1,0:T(1,128)}, u32[]{:S(2)}) copy-start(f32[8,1,256]{2,1,0:T(1,128)} %copy-done.14) | copy-start | bytes 24580
  646.8 197.2 %copy-start.19 = (f32[128]{0:T(128)S(1)}, f32[128]{0:T(128)}, u32[]{:S(2)}) copy-start(f32[128]{0:T(128)} %copy-done.18) | copy-start | bytes 1540
  646.8 197.2 %copy-start.21 = (f32[128]{0:T(128)S(1)}, f32[128]{0:T(128)}, u32[]{:S(2)}) copy-start(f32[128]{0:T(128)} %copy-done.20) | copy-start | bytes 1540
  646.8 1092.9 %reduce-scatter.17.cloned.1.call-start = ((), (), s32[]{:S(2)}) async-start(), calls=%async_computation.15 | async-start | bytes 37748736 | tf_op jit(solution)/shard_map/reduce_scatter | solution.py:51
  674.0 187.2 %copy-start.6 = (bf16[1,128,2048]{2,1,0:T(8,128)(2,1)S(1)}, bf16[1,128,2048]{2,1,0:T(8,128)(2,1)}, u32[]{:S(2)}) copy-start(bf16[1,128,2048]{2,1,0:T(8,128)(2,1)} %param.19) | copy-start | bytes 1572868
  933.7 1.0 copy-start.4
  933.7 926.4 %reduce-scatter.13.cloned.1.call-start = ((), (), s32[]{:S(2)}) async-start(), calls=%async_computation.13 | async-start | bytes 9437184 | tf_op jit(solution)/shard_map/reduce_scatter | solution.py:51
  940.5 1274.2 %reduce-scatter.15.cloned.1.call-start = ((), (), s32[]{:S(2)}) async-start(), calls=%async_computation.14 | async-start | bytes 37748736 | tf_op jit(solution)/shard_map/reduce_scatter | solution.py:51
  1273.9 111.0 %copy-start.23 = (f32[128,16]{0,1:T(8,128)S(1)}, f32[128,16]{0,1:T(8,128)}, u32[]{:S(2)}) copy-start(f32[128,16]{0,1:T(8,128)} %copy-done.22) | copy-start | bytes 24580
  1273.9 111.0 %copy-start.24 = (f32[128,16]{0,1:T(8,128)S(1)}, f32[128,16]{0,1:T(8,128)}, u32[]{:S(2)}) copy-start(f32[128,16]{0,1:T(8,128)} %get-tuple-element.226) | copy-start | bytes 24580
  1273.9 1209.2 %reduce-scatter.11.cloned.1.call-start = ((), (), s32[]{:S(2)}) async-start(), calls=%async_computation.12 | async-start | bytes 28311552 | tf_op jit(solution)/shard_map/reduce_scatter | solution.py:51
  1401.9 1229.4 %all-reduce.5.cloned.1.call-start = ((), (), s32[]{:S(2)}) async-start(), calls=%async_computation.18 | async-start | bytes 163840 | tf_op jit(solution)/shard_map/psum | solution.py:274
  1418.9 18.0 copy-start.29
  1418.9 19.1 copy-start.7
  1440.1 1471.6 %all-reduce.7.cloned.1.call-start = ((), (), s32[]{:S(2)}) async-start(), calls=%async_computation.19 | async-start | bytes 25165824 | tf_op jit(solution)/shard_map/psum | solution.py:57
  2483.1 0.7 copy-start.35
  2633.4 293.5 %copy-start.25 = (f32[256]{0:T(256)}, f32[256]{0:T(256)S(1)}, u32[]{:S(2)}) copy-start(f32[256]{0:T(256)S(1)} %dynamic_slice.49) | copy-start | bytes 3076
  2911.7 2.9 copy-start.11
  2914.6 3.5 copy-start.9
  2918.1 4.4 copy-start.8
  (2 other events, 1.2 us)
Sparse Core Ops, SparseCore 0:
  10.4 266.1 all-gather.11
  279.0 106.6 all-gather.17
  387.9 50.7 all-gather.13
  440.7 61.4 all-gather.15
  504.4 339.5 all-gather.19
  846.8 337.8 all-gather.21
  1187.1 95.0 reduce-scatter.18
  1285.2 97.5 reduce-scatter.20
  1386.7 352.8 reduce-scatter.16
  1744.0 116.1 reduce-scatter.12
  1864.1 350.6 reduce-scatter.14
  2218.6 264.4 reduce-scatter.10
  2491.0 140.2 all-reduce.4
  2634.6 277.0 all-reduce.6
where the time goes:
time: 2940 us; the launch traced here: 2930 us
  waiting for transfers between devices  2300 us (78%)
  matrix products  256 us (9%)
  local copies, waits for them, and re-layouts  187 us (6%)
  blocking collectives  123 us (4%)
  other arithmetic  51.4 us (2%)
    reduce_scatter x4, waiting for transfers between devices, reduce_rows(): lax.psum_scatter(term_fn(jnp.int32(0), own_rows * lax.axis_size('fsdp'))....  1040 us
    psum x1, waiting for transfers between devices, reduce_rows(): return lax.psum(shard_part, 'ctx').astype(jnp.float32)  274 us
    all_gather x1, waiting for transfers between devices, on_device(): lax.all_gather(w_fc2_rows, 'fsdp', axis=0, tiled=True)  244 us
    all_gather x1, waiting for transfers between devices, on_device(): lax.all_gather(w_qkv, 'fsdp', axis=0, tiled=True)  203 us
    all_gather x1, waiting for transfers between devices, on_device(): lax.all_gather(w_fc1, 'fsdp', axis=0, tiled=True)  170 us
    unnamed x16, waiting for transfers between devices  104 us
    psum x1, waiting for transfers between devices, on_device(): lax.psum((d_gain, d_shift, jnp.sum(d_projected.astype(jnp.float32), axis=...  92.3 us
    all_gather x1, waiting for transfers between devices, on_device(): lax.all_gather(w_dense, 'fsdp', axis=0, tiled=True)  80.4 us
  transfers between devices with their start and end apart: 14, of which 14 were waited for; matrix products, arithmetic and copies ran while one was open for 16% of the time, Pallas kernels for 0%

commit v1 on v0

v1 whole, which is shorter than its diff:
```python
import functools

import jax
import jax.numpy as jnp
from jax import lax
from jax.experimental import pallas as pl
from jax.experimental.pallas import tpu as pltpu
from jax.sharding import PartitionSpec as P

HEAD_DIM = 64
ROTARY = 32
NORM_EPS = 1e-05
ROPE_BASE = 10000.0
GELU_COEF = 0.7978845608028654
F32 = jnp.float32
BF16 = jnp.bfloat16
STRIP = 256
NT = (((1,), (1,)), ((), ()))
TN = (((0,), (0,)), ((), ()))


def attention_kernel(
    block, where, q_in, k_in, v_in, g_in, o_out, dq_out, dk_out, dv_out,
    qs, ks, vs, gs, os, dqs, dks, dvs, score, weight,
):
    rows = q_in.shape[0]
    blocks = rows // block

    def collect(at, carry):
        src = pl.ds(pl.multiple_of(where[at] * block, block), block)
        dst = pl.ds(pl.multiple_of(at * block, block), block)
        qs[dst, :] = q_in[src, :]
        ks[dst, :] = k_in[src, :]
        vs[dst, :] = v_in[src, :]
        gs[dst, :] = g_in[src, :]
        return carry

    lax.fori_loop(0, blocks, collect, 0)
    dks[...] = jnp.zeros_like(dks)
    dvs[...] = jnp.zeros_like(dvs)
    heads = q_in.shape[1] // HEAD_DIM
    scale = HEAD_DIM ** (-0.5)
    q_pos = lax.broadcasted_iota(jnp.int32, (STRIP, STRIP), 0)
    k_pos = lax.broadcasted_iota(jnp.int32, (STRIP, STRIP), 1)
    diagonal = k_pos <= q_pos
    for strip in range(rows // STRIP):
        here = slice(strip * STRIP, (strip + 1) * STRIP)
        for head in range(heads):
            cols = slice(head * HEAD_DIM, (head + 1) * HEAD_DIM)
            query = qs[here, cols] * jnp.asarray(scale, BF16)
            grad = gs[here, cols].astype(F32)
            peak = jnp.full((STRIP, 128), -1e30, F32)
            for chunk in range(strip + 1):
                there = slice(chunk * STRIP, (chunk + 1) * STRIP)
                part = lax.dot_general(query, ks[there, cols], NT, preferred_element_type=F32)
                if chunk == strip:
                    part = jnp.where(diagonal, part, -1e30)
                score[chunk] = part
                for lane in range(0, STRIP, 128):
                    peak = jnp.maximum(peak, part[:, lane : lane + 128])
            peak = jnp.max(peak, axis=1, keepdims=True)
            mass = jnp.zeros((STRIP, 128), F32)
            mixed = jnp.zeros((STRIP, HEAD_DIM), F32)
            for chunk in range(strip + 1):
                there = slice(chunk * STRIP, (chunk + 1) * STRIP)
                part = jnp.exp(score[chunk] - peak)
                score[chunk] = part
                for lane in range(0, STRIP, 128):
                    mass = mass + part[:, lane : lane + 128]
                low = part.astype(BF16)
                weight[chunk] = low
                mixed = mixed + jnp.dot(low, vs[there, cols], preferred_element_type=F32)
            inverse = 1.0 / jnp.sum(mass, axis=1, keepdims=True)
            mixed = mixed * inverse
            os[here, cols] = mixed.astype(BF16)
            grad = (grad * inverse).astype(BF16)
            centre = jnp.sum(grad.astype(F32) * mixed, axis=1, keepdims=True)
            d_query = jnp.zeros((STRIP, HEAD_DIM), F32)
            for chunk in range(strip + 1):
                there = slice(chunk * STRIP, (chunk + 1) * STRIP)
                part = lax.dot_general(grad, vs[there, cols], NT, preferred_element_type=F32)
                d_score = (score[chunk] * (part - centre)).astype(BF16)
                d_query = d_query + jnp.dot(d_score, ks[there, cols], preferred_element_type=F32)
                dks[there, cols] += lax.dot_general(
                    d_score, query, TN, preferred_element_type=F32
                )
                dvs[there, cols] += lax.dot_general(
                    weight[chunk], grad, TN, preferred_element_type=F32
                )
            dqs[here, cols] = d_query * scale

    def spread(at, carry):
        dst = pl.ds(pl.multiple_of(where[at] * block, block), block)
        src = pl.ds(pl.multiple_of(at * block, block), block)
        o_out[dst, :] = os[src, :]
        dq_out[dst, :] = dqs[src, :]
        dk_out[dst, :] = dks[src, :]
        dv_out[dst, :] = dvs[src, :]
        return carry

    lax.fori_loop(0, blocks, spread, 0)


def attention(where, block, queries, keys, values, grads):
    rows, width = queries.shape
    vmem = pl.BlockSpec(memory_space=pltpu.VMEM)
    smem = pl.BlockSpec(memory_space=pltpu.SMEM)
    wide = jax.ShapeDtypeStruct((rows, width), F32)
    chunks = rows // STRIP
    return pl.pallas_call(
        functools.partial(attention_kernel, block),
        out_shape=(jax.ShapeDtypeStruct((rows, width), BF16), wide, wide, wide),
        in_specs=[smem, vmem, vmem, vmem, vmem],
        out_specs=(vmem, vmem, vmem, vmem),
        scratch_shapes=[pltpu.VMEM((rows, width), BF16)] * 5
        + [pltpu.VMEM((rows, width), F32)] * 3
        + [pltpu.VMEM((chunks, STRIP, STRIP), F32), pltpu.VMEM((chunks, STRIP, STRIP), BF16)],
        compiler_params=pltpu.CompilerParams(vmem_limit_bytes=48 * 1024 * 1024),
        cost_estimate=pl.CostEstimate(
            flops=6 * rows * rows * width,
            bytes_accessed=rows * width * 22,
            transcendentals=rows * rows * width // HEAD_DIM // 2,
        ),
    )(where, queries, keys, values, grads)


def gelu_tanh(values):
    return (
        0.5 * values * (1.0 + jnp.tanh(GELU_COEF * (values + 0.044715 * values * values * values)))
    )


def turn_tables(positions, width):
    half = ROTARY // 2
    frequency = ROPE_BASE ** (-(jnp.arange(half, dtype=F32) * (2.0 / ROTARY)))
    turned = positions.astype(F32)[:, None] * frequency
    cosine, sine = jnp.cos(turned), jnp.sin(turned)
    rest = jnp.zeros((positions.shape[0], HEAD_DIM - ROTARY), F32)
    none = jnp.zeros_like(sine)
    heads = width // HEAD_DIM
    same = jnp.concatenate([cosine, cosine, rest + 1.0] * heads, axis=1)
    after = jnp.concatenate([-sine, none, rest] * heads, axis=1)
    before = jnp.concatenate([none, sine, rest] * heads, axis=1)
    return same, after, before


def turn(values, tables, back):
    same, after, before = tables
    half = ROTARY // 2
    moved = jnp.roll(values, -half, axis=1) * after + jnp.roll(values, half, axis=1) * before
    return values * same - moved if back else values * same + moved


def on_device(
    tokens, cotangent, block_order, positions, ln_gain, ln_bias, w_qkv, b_qkv, w_dense, b_dense,
    w_fc1, b_fc1, w_fc2, b_fc2,
):
    ctx, fsdp = lax.axis_size("ctx"), lax.axis_size("fsdp")
    c, f = lax.axis_index("ctx"), lax.axis_index("fsdp")
    share = ctx // fsdp
    rows, width = tokens.shape[1:]
    seq = rows * ctx
    ff = w_fc1.shape[1]
    own_width, own_ff = width // ctx, ff // ctx
    own_rows = width // fsdp
    tokens = tokens.reshape(rows, width)
    cotangent = cotangent.reshape(rows, width)
    swap = [
        (cs * fsdp + fs, (share * fs + cs % share) * fsdp + cs // share)
        for cs in range(ctx)
        for fs in range(fsdp)
    ]

    small = jnp.concatenate([ln_gain, ln_bias, b_qkv, b_fc1, b_dense, b_fc2])
    small = lax.all_gather(small, "fsdp", axis=0)
    small_at, at = [], 0
    for piece in (ln_gain, ln_bias, b_qkv, b_fc1, b_dense, b_fc2):
        small_at.append(small[:, at : at + piece.shape[0]].reshape(-1).astype(F32))
        at += piece.shape[0]
    gain, shift, bias_qkv, bias_fc1, bias_dense, bias_fc2 = small_at
    in_rows = jnp.concatenate(
        [
            lax.dynamic_slice_in_dim(w_qkv, part * width + c * own_width, own_width, 1)
            for part in range(3)
        ]
        + [lax.dynamic_slice_in_dim(w_fc1, c * own_ff, own_ff, 1)],
        axis=1,
    )
    w_in = lax.all_gather(in_rows, "fsdp", axis=0, tiled=True)
    out_rows = jnp.concatenate(
        [
            lax.dynamic_slice_in_dim(w_dense, lax.rem(c, share) * own_width, own_width, 0),
            lax.dynamic_slice_in_dim(w_fc2, lax.rem(c, share) * own_ff, own_ff, 0),
        ],
        axis=0,
    )
    w_out = lax.ppermute(out_rows, ("ctx", "fsdp"), swap)
    own_bias_qkv = jnp.concatenate(
        [
            lax.dynamic_slice_in_dim(bias_qkv, part * width + c * own_width, own_width, 0)
            for part in range(3)
        ]
    )
    own_bias_fc1 = lax.dynamic_slice_in_dim(bias_fc1, c * own_ff, own_ff, 0)

    x_all = lax.all_gather(tokens, "ctx", axis=0, tiled=True)
    g_all = lax.all_gather(cotangent, "ctx", axis=0, tiled=True)
    pos_all = lax.all_gather(positions.reshape(rows), "ctx", axis=0, tiled=True)
    x_f = x_all.astype(F32)
    mean = jnp.mean(x_f, axis=1, keepdims=True)
    centred = x_f - mean
    inverse = lax.rsqrt(jnp.mean(centred * centred, axis=1, keepdims=True) + NORM_EPS)
    hidden = (centred * inverse * gain + shift).astype(BF16)

    cut = 3 * own_width
    projected = jnp.dot(hidden, w_in[:, :cut], preferred_element_type=F32) + own_bias_qkv
    up_value = jnp.dot(hidden, w_in[:, cut:], preferred_element_type=F32) + own_bias_fc1
    activated = gelu_tanh(up_value).astype(BF16)
    tables = turn_tables(pos_all, own_width)
    queries = turn(projected[:, :own_width], tables, False).astype(BF16)
    keys = turn(projected[:, own_width : 2 * own_width], tables, False).astype(BF16)
    values = projected[:, 2 * own_width :].astype(BF16)
    d_attended = lax.dot_general(g_all, w_out[:own_width], NT, preferred_element_type=F32)
    d_attended = d_attended.astype(BF16)
    d_act = lax.dot_general(g_all, w_out[own_width:], NT, preferred_element_type=F32)
    d_up = jax.vjp(gelu_tanh, up_value)[1](d_act)[0].astype(BF16)

    def scatter(term):
        return lax.psum_scatter(term.astype(BF16), "fsdp", scatter_dimension=0, tiled=True)

    def from_ctx(piece):
        return lax.all_gather(piece, "ctx", axis=0)

    def swapped(piece):
        return from_ctx(lax.ppermute(piece, ("ctx", "fsdp"), swap))

    def rows_of(pieces, amount):
        pieces = pieces.astype(F32).reshape(fsdp, share, amount // fsdp, width)
        return pieces.transpose(1, 0, 2, 3).reshape(share * amount, width)

    grad_fc1 = from_ctx(scatter(lax.dot_general(hidden, d_up, TN, preferred_element_type=F32)))
    grad_fc2 = swapped(scatter(lax.dot_general(activated, g_all, TN, preferred_element_type=F32)))

    blocks = block_order.shape[0]
    where = jnp.argsort(block_order).astype(jnp.int32)
    attended, d_query, d_key, d_value = attention(
        where, seq // blocks, queries, keys, values, d_attended
    )
    d_projected = jnp.concatenate(
        [turn(d_query, tables, True), turn(d_key, tables, True), d_value], axis=1
    ).astype(BF16)

    grad_qkv = from_ctx(
        scatter(lax.dot_general(hidden, d_projected, TN, preferred_element_type=F32))
    )
    grad_dense = swapped(scatter(lax.dot_general(attended, g_all, TN, preferred_element_type=F32)))

    branches = jnp.dot(attended, w_out[:own_width], preferred_element_type=F32) + jnp.dot(
        activated, w_out[own_width:], preferred_element_type=F32
    )
    branches = lax.psum_scatter(branches.astype(BF16), "ctx", scatter_dimension=0, tiled=True)
    x_own = tokens.astype(F32)
    result = x_own + branches.astype(F32) + bias_dense + bias_fc2

    d_hidden = lax.dot_general(
        d_projected, w_in[:, :cut], NT, preferred_element_type=F32
    ) + lax.dot_general(d_up, w_in[:, cut:], NT, preferred_element_type=F32)
    part_gain = jnp.sum(d_hidden * (centred * inverse), axis=0)
    part_shift = jnp.sum(d_hidden, axis=0)
    d_hidden = lax.psum_scatter(
        d_hidden.astype(BF16), "ctx", scatter_dimension=0, tiled=True
    ).astype(F32)
    own_mean = jnp.mean(x_own, axis=1, keepdims=True)
    own_centred = x_own - own_mean
    own_inverse = lax.rsqrt(jnp.mean(own_centred * own_centred, axis=1, keepdims=True) + NORM_EPS)
    normed = own_centred * own_inverse
    scaled = d_hidden * gain
    input_grad = cotangent.astype(F32) + own_inverse * (
        scaled
        - jnp.mean(scaled, axis=1, keepdims=True)
        - normed * jnp.mean(scaled * normed, axis=1, keepdims=True)
    )

    vector = jnp.concatenate(
        [
            part_gain,
            part_shift,
            jnp.sum(cotangent.astype(F32), axis=0),
            jnp.sum(d_projected.astype(F32), axis=0),
            jnp.sum(d_up.astype(F32), axis=0),
        ]
    )
    vector = lax.all_gather(vector, "ctx", axis=0)
    sums = jnp.sum(vector[:, : 3 * width], axis=0)
    columns = vector[:, 3 * width : 3 * width + cut].reshape(ctx, 3, own_width)
    columns = columns.transpose(1, 0, 2).reshape(3 * width)
    units = vector[:, 3 * width + cut :].reshape(ff)
    pieces = [sums[:width], sums[width : 2 * width], sums[2 * width :], columns, units]
    pieces = jnp.concatenate([piece.reshape(fsdp, -1) for piece in pieces], axis=1)
    pieces = lax.psum_scatter(pieces, "fsdp", scatter_dimension=0, tiled=True).reshape(-1)
    cuts = [own_rows, 2 * own_rows, 3 * own_rows, 3 * own_rows + 3 * width // fsdp]
    d_gain, d_shift, d_bias, d_bias_qkv, d_bias_fc1 = jnp.split(pieces, cuts)

    out_fc1 = grad_fc1.transpose(1, 0, 2).astype(F32).reshape(own_rows, ff)
    out_qkv = grad_qkv.reshape(ctx, own_rows, 3, own_width).transpose(1, 2, 0, 3)
    out_qkv = out_qkv.astype(F32).reshape(own_rows, 3 * width)
    return (
        result.astype(BF16).reshape(1, rows, width),
        input_grad.reshape(1, rows, width),
        d_gain,
        d_shift,
        out_qkv,
        d_bias_qkv,
        rows_of(grad_dense, own_width),
        d_bias,
        out_fc1,
        d_bias_fc1,
        rows_of(grad_fc2, own_ff),
        d_bias,
    )


def solution(mesh):
    split = P("fsdp", "ctx", None)
    matrix = P("fsdp", None)
    vector = P("fsdp")
    return jax.shard_map(
        on_device,
        mesh=mesh,
        in_specs=(split, split, P(), P("fsdp", "ctx"), vector, vector)
        + (matrix, vector) * 4,
        out_specs=(split, split, vector, vector) + (matrix, vector) * 4,
        check_vma=False,
    )
```

time: 2940 us -> 1110 us (0.38)
  waiting for transfers between devices: 2300 us -> 634 us
  matrix products: 256 us -> 114 us
  local copies, waits for them, and re-layouts: 187 us -> 74.7 us
  Pallas kernels: 0 us -> 36.6 us
  blocking collectives: 123 us -> 157 us
    reduce_scatter x4 -> x6, waiting for transfers between devices: 1040 us -> 390 us  [the longest x4 199 us: scatter(): lax.psum_scatter(term.astype(BF16), 'fsdp', scatter_dimension=0, tiled=True)]
    all_gather x6 -> x7, waiting for transfers between devices: 795 us -> 194 us  [the longest x4 115 us: from_ctx(): return lax.all_gather(piece, 'ctx', axis=0)]
    psum x2 -> x0, waiting for transfers between devices: 367 us -> none  [the longest x1 274 us: reduce_rows(): return lax.psum(shard_part, 'ctx').astype(jnp.float32)]
    dot_general x40 -> x12, matrix products: 256 us -> 114 us  [the longest x1 14.8 us: on_device(): lax.dot_general(d_projected, w_in[:, :cut], NT, preferred_element_type=F32)]
    convert_element_type x2 -> x1, local copies, waits for them, and re-layouts: 55.5 us -> 0.01 us  [on_device(): small_at.append(small[:, at:at + piece.shape[0]].reshape(-1).astype(F32))]
    unnamed x16 -> x15, waiting for transfers between devices: 104 us -> 50 us
    reshape x3 -> x6, local copies, waits for them, and re-layouts: 71.1 us -> 21.8 us  [the longest x2 11.9 us: on_device(): out_qkv = out_qkv.astype(F32).reshape(own_rows, 3 * width)]
    pallas_call x0 -> x1, Pallas kernels: none -> 36.6 us  [attention(): pl.pallas_call(functools.partial(attention_kernel, block), out_shape=(jax...]
  transfers between devices with their start and end apart: 14 -> 17, of which waited for: 14 -> 12; matrix products, arithmetic and copies ran while one was open for 16% -> 19% of each run, Pallas kernels for 0% -> 0%
where the time goes in v1:
time: 1110 us; the launch traced here: 1100 us
  waiting for transfers between devices  634 us (57%)
  blocking collectives  157 us (14%)
  matrix products  114 us (10%)
  local copies, waits for them, and re-layouts  74.7 us (7%)
  other arithmetic  43.7 us (4%)
  Pallas kernels  36.6 us (3%)
  starting transfers between devices  25.4 us (2%)
  between operations  14.9 us (1%)
    reduce_scatter x4, waiting for transfers between devices, scatter(): lax.psum_scatter(term.astype(BF16), 'fsdp', scatter_dimension=0, tiled=True)  199 us
    all_gather x4, waiting for transfers between devices, from_ctx(): return lax.all_gather(piece, 'ctx', axis=0)  115 us
    all_gather x1, blocking collectives, on_device(): pos_all = lax.all_gather(positions.reshape(rows), 'ctx', axis=0, tiled=True)  107 us
    reduce_scatter x1, waiting for transfers between devices, on_device(): lax.psum_scatter(branches.astype(BF16), 'ctx', scatter_dimension=0, tiled...  98.4 us
    reduce_scatter x1, waiting for transfers between devices, on_device(): lax.psum_scatter(d_hidden.astype(BF16), 'ctx', scatter_dimension=0, tiled...  91.8 us
    unnamed x15, waiting for transfers between devices  50 us
    all_gather x1, waiting for transfers between devices, on_device(): g_all = lax.all_gather(cotangent, 'ctx', axis=0, tiled=True)  39.7 us
    all_gather x1, waiting for transfers between devices, on_device(): w_in = lax.all_gather(in_rows, 'fsdp', axis=0, tiled=True)  39.5 us
  transfers between devices with their start and end apart: 17, of which 12 were waited for; matrix products, arithmetic and copies ran while one was open for 19% of the time, Pallas kernels for 0%

profile of v1, /device:TPU:1, one launch (start us, length us, event | category | flops | bytes accessed | tf_op | source)
XLA Modules:
  0.0 1100.7 jit_solution(806112602940701577)
XLA Ops:
  15.1 21.2 %collective-permute-start = (bf16[640,2048]{1,0:T(8,128)(2,1)}, bf16[640,2048]{1,0:T(8,128)(2,1)}, u32[]{:S(2)}, u32[]{:S(2)}) collective-permute-start(bf16[640,2048]{1,0:T(8,128)(2,1)} %pad_maximum_fusion), channel_id=1, source_target_pairs={{0,0},{1,16},{2,32},{3,48},{4,64},{5,80},{6,96},{7,112},{8,8},{9,2... | collective-permute-start | bytes 7864328 | tf_op jit(solution)/shard_map/ppermute | solution.py:197
  37.5 107.2 %all-gather.2 = s32[1,2048]{1,0:T(1,128)S(1)} all-gather(s32[1,128]{1,0:T(1,128)S(1)} %copy-done.28), channel_id=4, replica_groups=mesh['ctx'=16,'fsdp'=8] {'ctx'}, dimensions={1}, use_global_device_ids=true | all-gather | bytes 8704 | tf_op jit(solution)/shard_map/all_gather | solution.py:208
  144.7 29.8 %all-gather.9 = bf16[8,1,2816]{2,1,0:T(2,128)(2,1)S(1)} all-gather(bf16[1,1,2816]{2,1,0:T(2,128)(2,1)S(1)} %reshape.253), channel_id=3, replica_groups=mesh['ctx'=16,'fsdp'=8] {'fsdp'}, dimensions={0}, use_global_device_ids=true | all-gather | bytes 50688 | tf_op jit(solution)/shard_map/all_gather | solution.py:175
  175.3 5.5 multiply_sine_fusion
  181.0 4.4 concatenate.64
  185.4 4.4 concatenate.62
  191.4 2.2 concatenate.60
  193.8 4.9 convert_reduce_fusion
  199.9 2.3 fusion.8
  202.2 5.4 fusion.6
  207.6 39.5 %all-gather.19.cloned.1.call-done = bf16[2048,896]{1,0:T(8,128)(2,1)} async-done(((bf16[256,896]{1,0:T(8,128)(2,1)}), bf16[2048,896]{1,0:T(8,128)(2,1)}) %all-gather.19.cloned.1.call-update) | async-done | bytes 3670032 | tf_op jit(solution)/shard_map/all_gather | solution.py:189
  247.1 7.8 convolution_add_fusion.1
  259.9 39.7 %all-gather.23.cloned.1.call-done = bf16[1,2048,2048]{2,1,0:T(8,128)(2,1)} async-done(((bf16[1,128,2048]{2,1,0:T(8,128)(2,1)}), bf16[1,2048,2048]{2,1,0:T(8,128)(2,1)}) %all-gather.23.cloned.1.call-update) | async-done | bytes 8388624 | tf_op jit(solution)/shard_map/all_gather | solution.py:207
  299.6 6.0 fusion.35.g_in
  306.6 36.6 %shard_map.229 = (bf16[2048,128]{1,0:T(8,128)(2,1)S(1)}, f32[2048,128]{1,0:T(8,128)S(1)}, f32[2048,128]{1,0:T(8,128)S(1)}, f32[2048,128]{1,0:T(8,128)S(1)}) custom-call(s32[32]{0:T(128)S(1)} %get-tuple-element.17.where, bf16[2048,128]{1,0:T(8,128)(2,1)S(1)} %copy-done.2, bf16[2048,128]{1,0:T(8,128)(2,1)S(1)} %get-tuple-element.63.k_in, ...), custom_call_target="tpu_custom_call" | custom-call | flops 3221225472 | bytes 5767168 | tf_op jit(solution)/shard_map/pallas_call | solution.py:110
  343.2 2.7 fusion.85
  345.9 2.7 fusion.84
  352.1 5.5 fusion.72
  358.5 9.1 convolution_convert_fusion.1
  367.8 7.7 fusion.45
  375.6 12.4 %convert_reduce_fusion.1 = (f32[512]{0:T(512)S(1)}, bf16[2048,512]{1,0:T(8,128)(2,1)S(1)}) fusion(bf16[1,2048,2048]{2,1,0:T(8,128)(2,1)} %all-gather.23.cloned.1.call-done, bf16[640,2048]{1,0:T(8,128)(2,1)} %collective-permute-done, f32[2048,512]{1,0:T(8,128)S(1)} %fusion.45, f32[512]{0:T(512)S(1)} %dynamic_slice.39), kind=kOutput, calls=%fused_computation.38 | convolution fusion | flops 4323278336 | bytes 16781312 | tf_op jit(solution)/shard_map/dot_general | solution.py:225
  389.3 5.7 convolution_convert_fusion
  395.2 11.2 %fusion.26 = bf16[512,2048]{1,0:T(8,128)(2,1)} fusion(bf16[1,2048,2048]{2,1,0:T(8,128)(2,1)} %all-gather.23.cloned.1.call-done, f32[2048,512]{1,0:T(8,128)} %copy-done.32, f32[512]{0:T(512)S(1)} %dynamic_slice.39), kind=kOutput, calls=%fused_computation.41 | convolution fusion | flops 4306501632 | bytes 14682112 | tf_op jit(solution)/shard_map/dot_general | solution.py:242
  406.9 12.5 %fusion.43 = f32[2048,2048]{1,0:T(8,128)} fusion(bf16[2048,512]{1,0:T(8,128)(2,1)} %copy-done.31, bf16[2048,896]{1,0:T(8,128)(2,1)} %all-gather.19.cloned.1.call-done), kind=kOutput, calls=%fused_computation.53 | convolution fusion | flops 4294967296 | bytes 20971520 | tf_op jit(solution)/shard_map/dot_general | solution.py:267
  419.4 14.8 %fusion.81 = (f32[2048]{0:T(1024)S(1)}, f32[2048]{0:T(1024)S(1)}, bf16[2048,2048]{1,0:T(8,128)(2,1)}) fusion(f32[2048]{0:T(1024)S(1)} %add_rsqrt_fusion, f32[2048]{0:T(1024)S(1)} %broadcast_multiply_fusion, bf16[1,2048,2048]{2,1,0:T(8,128)(2,1)} %all-gather.21.cloned.1.call-done, f32[2048,2048]{1,0:T(8,128)} %fusion.43, ...), kind=kOutput, calls=%fused_computation.147 | convolution fusion | flops 3259494400 | bytes 36732928 | tf_op jit(solution)/shard_map/dot_general | solution.py:265
  434.7 20.2 %all-gather.10 = f32[16,1,7040]{2,1,0:T(1,128)S(1)} all-gather(f32[1,1,7040]{2,1,0:T(1,128)S(1)} %reshape.255), channel_id=6, replica_groups=mesh['ctx'=16,'fsdp'=8] {'ctx'}, dimensions={0}, use_global_device_ids=true | all-gather | bytes 478720 | tf_op jit(solution)/shard_map/all_gather | solution.py:293
  458.1 42.9 %reduce-scatter.11.cloned.1.call-done = bf16[256,384]{1,0:T(8,128)(2,1)} async-done(((bf16[2048,384]{1,0:T(8,128)(2,1)}), bf16[256,384]{1,0:T(8,128)(2,1)}) %reduce-scatter.11.cloned.1.call-update) | async-done | bytes 196624 | tf_op jit(solution)/shard_map/reduce_scatter | solution.py:229
  501.0 78.3 %reduce-scatter.15.cloned.1.call-done = bf16[256,512]{1,0:T(8,128)(2,1)} async-done(((bf16[2048,512]{1,0:T(8,128)(2,1)}), bf16[256,512]{1,0:T(8,128)(2,1)}) %reduce-scatter.15.cloned.1.call-update) | async-done | bytes 262160 | tf_op jit(solution)/shard_map/reduce_scatter | solution.py:229
  579.4 78.1 %reduce-scatter.17.cloned.1.call-done = bf16[64,2048]{1,0:T(8,128)(2,1)} async-done(((bf16[512,2048]{1,0:T(8,128)(2,1)}), bf16[64,2048]{1,0:T(8,128)(2,1)}) %reduce-scatter.17.cloned.1.call-update) | async-done | bytes 262160 | tf_op jit(solution)/shard_map/reduce_scatter | solution.py:229
  660.7 13.7 %fusion.41 = f32[2048,2048]{1,0:T(8,128)} fusion(bf16[640,2048]{1,0:T(8,128)(2,1)} %collective-permute-done, f32[2048,512]{1,0:T(8,128)} %copy-done.32, f32[512]{0:T(512)S(1)} %dynamic_slice.39), kind=kOutput, calls=%fused_computation.51 | convolution fusion | flops 4305453056 | bytes 23070720 | tf_op jit(solution)/shard_map/dot_general | solution.py:258
  674.3 11.6 %add_convert_fusion = bf16[2048,2048]{1,0:T(8,128)(2,1)} fusion(f32[2048,2048]{1,0:T(8,128)} %fusion.41, bf16[2048,128]{1,0:T(8,128)(2,1)S(1)} %get-tuple-element.18, bf16[640,2048]{1,0:T(8,128)(2,1)} %collective-permute-done), kind=kOutput, calls=%fused_computation.11 | convolution fusion | flops 1082130432 | bytes 26214400 | tf_op jit(solution)/shard_map/dot_general | solution.py:258
  687.7 47.8 %all-reduce.3.cloned.1.call-done = f32[8,2560]{1,0:T(8,128)} async-done(((f32[8,2560]{1,0:T(8,128)}), f32[8,2560]{1,0:T(8,128)}) %all-reduce.3.cloned.1.call-update) | async-done | bytes 81936
  737.6 2.1 dynamic-slice.6
  741.7 33.5 %all-gather.27.cloned.1.call-done = bf16[256,2048]{1,0:T(8,128)(2,1)} async-done(((bf16[16,2048]{1,0:T(8,128)(2,1)}), bf16[256,2048]{1,0:T(8,128)(2,1)}) %all-gather.27.cloned.1.call-update) | async-done | bytes 1048592 | tf_op jit(solution)/shard_map/all_gather | solution.py:232
  778.2 34.4 %all-gather.25.cloned.1.call-done = bf16[4096,384]{1,0:T(8,128)(2,1)} async-done(((bf16[256,384]{1,0:T(8,128)(2,1)}), bf16[4096,384]{1,0:T(8,128)(2,1)}) %all-gather.25.cloned.1.call-update) | async-done | bytes 3145744 | tf_op jit(solution)/shard_map/all_gather | solution.py:232
  812.6 5.5 copy.66
  818.2 5.6 copy.83
  823.8 6.3 copy.67
  830.1 6.6 copy.71
  836.7 15.3 %all-gather.29.cloned.1.call-done = bf16[4096,512]{1,0:T(8,128)(2,1)} async-done(((bf16[256,512]{1,0:T(8,128)(2,1)}), bf16[4096,512]{1,0:T(8,128)(2,1)}) %all-gather.29.cloned.1.call-update) | async-done | bytes 4194320 | tf_op jit(solution)/shard_map/all_gather | solution.py:232
  852.0 3.4 convert_bitcast_fusion.2
  855.4 4.4 copy.77
  859.8 31.8 %all-gather.31.cloned.1.call-done = bf16[1024,2048]{1,0:T(8,128)(2,1)} async-done(((bf16[64,2048]{1,0:T(8,128)(2,1)}), bf16[1024,2048]{1,0:T(8,128)(2,1)}) %all-gather.31.cloned.1.call-update) | async-done | bytes 4194320 | tf_op jit(solution)/shard_map/all_gather | solution.py:232
  891.6 3.2 convert_bitcast_fusion.1
  894.9 4.0 copy.70
  898.9 91.8 %reduce-scatter.9.cloned.1.call-done = bf16[128,2048]{1,0:T(8,128)(2,1)} async-done(((bf16[2048,2048]{1,0:T(8,128)(2,1)}), bf16[128,2048]{1,0:T(8,128)(2,1)}) %reduce-scatter.9.cloned.1.call-update) | async-done | bytes 524304 | tf_op jit(solution)/shard_map/reduce_scatter | solution.py:270
  992.0 98.4 %reduce-scatter.7.cloned.1.call-done = bf16[128,2048]{1,0:T(8,128)(2,1)} async-done(((bf16[2048,2048]{1,0:T(8,128)(2,1)}), bf16[128,2048]{1,0:T(8,128)(2,1)}) %reduce-scatter.7.cloned.1.call-update) | async-done | bytes 524304 | tf_op jit(solution)/shard_map/reduce_scatter | solution.py:261
  1090.4 3.0 fusion.59
  (191 shorter events, 42.9 us)
Async XLA Ops:
  7.2 4.4 copy-start
  7.2 186.6 %all-gather.21.cloned.1.call-start = ((), (), s32[]{:S(2)}) async-start(), calls=%async_computation.13 | async-start | bytes 8912896 | tf_op jit(solution)/shard_map/all_gather | solution.py:206
  7.9 239.2 %all-gather.19.cloned.1.call-start = ((), (), s32[]{:S(2)}) async-start(), calls=%async_computation.6 | async-start | bytes 4128768 | tf_op jit(solution)/shard_map/all_gather | solution.py:189
  10.7 288.9 %all-gather.23.cloned.1.call-start = ((), (), s32[]{:S(2)}) async-start(), calls=%async_computation.14 | async-start | bytes 8912896 | tf_op jit(solution)/shard_map/all_gather | solution.py:207
  11.5 444.4 %reduce-scatter.13.cloned.1.call-start = ((), (), s32[]{:S(2)}) async-start(), calls=%async_computation.10 | async-start | bytes 589824 | tf_op jit(solution)/shard_map/reduce_scatter | solution.py:229
  11.6 24.7 %copy-start.24 = (bf16[256]{0:T(256)(128)(2,1)S(1)}, bf16[256]{0:T(256)(128)(2,1)}, u32[]{:S(2)}) copy-start(bf16[256]{0:T(256)(128)(2,1)} %param.18) | copy-start | bytes 1540
  11.6 24.9 %copy-start.25 = (bf16[256]{0:T(256)(128)(2,1)S(1)}, bf16[256]{0:T(256)(128)(2,1)}, u32[]{:S(2)}) copy-start(bf16[256]{0:T(256)(128)(2,1)} %param.19) | copy-start | bytes 1540
  11.6 25.1 %copy-start.22 = (bf16[768]{0:T(1024)(128)(2,1)S(1)}, bf16[768]{0:T(1024)(128)(2,1)}, u32[]{:S(2)}) copy-start(bf16[768]{0:T(1024)(128)(2,1)} %param.21) | copy-start | bytes 4612
  11.6 25.3 %copy-start.23 = (bf16[1024]{0:T(1024)(128)(2,1)S(1)}, bf16[1024]{0:T(1024)(128)(2,1)}, u32[]{:S(2)}) copy-start(bf16[1024]{0:T(1024)(128)(2,1)} %param.25) | copy-start | bytes 6148
  11.6 25.5 %copy-start.26 = (bf16[256]{0:T(256)(128)(2,1)S(1)}, bf16[256]{0:T(256)(128)(2,1)}, u32[]{:S(2)}) copy-start(bf16[256]{0:T(256)(128)(2,1)} %param.23) | copy-start | bytes 1540
  11.7 25.7 %copy-start.27 = (bf16[256]{0:T(256)(128)(2,1)S(1)}, bf16[256]{0:T(256)(128)(2,1)}, u32[]{:S(2)}) copy-start(bf16[256]{0:T(256)(128)(2,1)} %param.27) | copy-start | bytes 1540
  11.7 25.9 %copy-start.28 = (s32[1,128]{1,0:T(1,128)S(1)}, s32[1,128]{1,0:T(1,128)}, u32[]{:S(2)}) copy-start(s32[1,128]{1,0:T(1,128)} %param.17) | copy-start | bytes 1540
  15.1 244.8 %collective-permute-start = (bf16[640,2048]{1,0:T(8,128)(2,1)}, bf16[640,2048]{1,0:T(8,128)(2,1)}, u32[]{:S(2)}, u32[]{:S(2)}) collective-permute-start(bf16[640,2048]{1,0:T(8,128)(2,1)} %pad_maximum_fusion), channel_id=1, source_target_pairs={{0,0},{1,16},{2,32},{3,48},{4,64},{5,80},{6,96},{7,112},{8,8},{9,2... | collective-permute-start | bytes 7864328 | tf_op jit(solution)/shard_map/ppermute | solution.py:197
  175.3 26.9 %copy-start.15 = (f32[1,2,8,128]{3,1,2,0:T(2,128)}, f32[1,2,8,128]{3,1,2,0:T(2,128)S(1)}, u32[]{:S(2)}) copy-start(f32[1,2,8,128]{3,1,2,0:T(2,128)S(1)} %copy.78) | copy-start | bytes 24580
  185.4 4.4 copy-start.29
  193.7 63.5 %copy-start.8 = (f32[2048,128]{1,0:T(8,128)}, f32[2048,128]{1,0:T(8,128)S(1)}, u32[]{:S(2)}) copy-start(f32[2048,128]{1,0:T(8,128)S(1)} %concatenate.60) | copy-start | bytes 3145732
  193.8 6.1 copy-start.4
  256.4 1.2 copy-start.6
  256.5 1.5 copy-start.7
  299.6 6.0 copy-start.2
  305.6 1.0 copy-start.3
  343.2 5.5 slice-start
  345.9 4.0 slice-start.1
  352.0 149.0 %reduce-scatter.11.cloned.1.call-start = ((), (), s32[]{:S(2)}) async-start(), calls=%async_computation.9 | async-start | bytes 1769472 | tf_op jit(solution)/shard_map/reduce_scatter | solution.py:229
  357.5 0.8 copy-start.10
  357.5 1.0 copy-start.12
  367.6 211.8 %reduce-scatter.15.cloned.1.call-start = ((), (), s32[]{:S(2)}) async-start(), calls=%async_computation.11 | async-start | bytes 2359296 | tf_op jit(solution)/shard_map/reduce_scatter | solution.py:229
  367.8 21.5 %slice-start.2 = ((s8[8388608]{0:T(1024)(128)(4,1)}), s8[4194304]{0:T(1024)(128)(4,1)S(1)}, s32[]{:S(2)}) async-start(s8[8388608]{0:T(1024)(128)(4,1)} %bitcast.165), calls=%async_computation.22 | async-start | bytes 8388608
  375.6 12.4 %copy-start.32 = (f32[2048,512]{1,0:T(8,128)}, f32[2048,512]{1,0:T(8,128)S(1)}, u32[]{:S(2)}) copy-start(f32[2048,512]{1,0:T(8,128)S(1)} %fusion.45) | copy-start | bytes 12582916
  375.6 13.7 %slice-start.3 = ((s8[8388608]{0:T(1024)(128)(4,1)}), s8[4194304]{0:T(1024)(128)(4,1)S(1)}, s32[]{:S(2)}) async-start(s8[8388608]{0:T(1024)(128)(4,1)} %bitcast.165), calls=%async_computation.23 | async-start | bytes 8388608
  388.0 1.3 copy-start.31
  389.3 5.8 copy-start.9
  395.1 262.5 %reduce-scatter.17.cloned.1.call-start = ((), (), s32[]{:S(2)}) async-start(), calls=%async_computation.12 | async-start | bytes 2359296 | tf_op jit(solution)/shard_map/reduce_scatter | solution.py:229
  406.4 13.0 %copy-start.11 = (bf16[2048,128]{1,0:T(8,128)(2,1)S(1)}, bf16[2048,128]{1,0:T(8,128)(2,1)}, u32[]{:S(2)}) copy-start(bf16[2048,128]{1,0:T(8,128)(2,1)} %copy-done.10) | copy-start | bytes 1572868
  406.4 13.0 %copy-start.13 = (bf16[2048,128]{1,0:T(8,128)(2,1)S(1)}, bf16[2048,128]{1,0:T(8,128)(2,1)}, u32[]{:S(2)}) copy-start(bf16[2048,128]{1,0:T(8,128)(2,1)} %copy-done.12) | copy-start | bytes 1572868
  406.4 329.1 %all-reduce.3.cloned.1.call-start = ((), (), s32[]{:S(2)}) async-start(), calls=%async_computation.19 | async-start | bytes 163840
  455.8 319.5 %all-gather.27.cloned.1.call-start = ((), (), s32[]{:S(2)}) async-start(), calls=%async_computation.16 | async-start | bytes 1114112 | tf_op jit(solution)/shard_map/all_gather | solution.py:232
  455.9 1.5 collective-permute-start.1
  458.0 354.6 %all-gather.25.cloned.1.call-start = ((), (), s32[]{:S(2)}) async-start(), calls=%async_computation.15 | async-start | bytes 3342336 | tf_op jit(solution)/shard_map/all_gather | solution.py:232
  501.0 351.0 %all-gather.29.cloned.1.call-start = ((), (), s32[]{:S(2)}) async-start(), calls=%async_computation.17 | async-start | bytes 4456448 | tf_op jit(solution)/shard_map/all_gather | solution.py:232
  579.4 312.2 %all-gather.31.cloned.1.call-start = ((), (), s32[]{:S(2)}) async-start(), calls=%async_computation.18 | async-start | bytes 4456448 | tf_op jit(solution)/shard_map/all_gather | solution.py:232
  657.6 1.6 collective-permute-start.2
  659.9 330.7 %reduce-scatter.9.cloned.1.call-start = ((), (), s32[]{:S(2)}) async-start(), calls=%async_computation.8 | async-start | bytes 8912896 | tf_op jit(solution)/shard_map/reduce_scatter | solution.py:270
  660.6 429.8 %reduce-scatter.7.cloned.1.call-start = ((), (), s32[]{:S(2)}) async-start(), calls=%async_computation.7 | async-start | bytes 8912896 | tf_op jit(solution)/shard_map/reduce_scatter | solution.py:261
  685.9 1.3 copy-start.5
  737.6 355.8 %copy-start.21 = (f32[1,256]{1,0:T(1,128)}, f32[1,256]{1,0:T(1,128)S(1)}, u32[]{:S(2)}) copy-start(f32[1,256]{1,0:T(1,128)S(1)} %get-tuple-element.88) | copy-start | bytes 3076
  894.8 95.8 %copy-start.16 = (f32[1,2,8,128]{3,1,2,0:T(2,128)S(1)}, f32[1,2,8,128]{3,1,2,0:T(2,128)}, u32[]{:S(2)}) copy-start(f32[1,2,8,128]{3,1,2,0:T(2,128)} %copy-done.15) | copy-start | bytes 24580
  894.9 199.1 %copy-start.1 = (bf16[256,2048]{1,0:T(8,128)(2,1)S(1)}, bf16[256,2048]{1,0:T(8,128)(2,1)}, u32[]{:S(2)}) copy-start(bf16[256,2048]{1,0:T(8,128)(2,1)} %param.22) | copy-start | bytes 3145732
  (6 other events, 4.1 us)
Sparse Core Ops, SparseCore 0:
  9.7 164.2 all-gather.20
  176.9 70.1 all-gather.18
  248.8 50.7 all-gather.22
  352.1 69.2 reduce-scatter.12
  425.4 75.4 reduce-scatter.10
  505.6 73.6 reduce-scatter.14
  583.7 73.8 reduce-scatter.16
  660.8 74.7 all-reduce.2
  737.8 37.4 all-gather.26
  776.8 35.7 all-gather.24
  814.4 37.5 all-gather.28
  854.1 37.4 all-gather.30
  894.0 96.5 reduce-scatter.8
  992.9 97.5 reduce-scatter.6

commit v2 on v1

--- a/solution.py
+++ b/solution.py
@@ -124,6 +124,467 @@
     )(where, queries, keys, values, grads)
 
 
+MESH = pl.DeviceIdType.MESH
+
+
+class Place:
+    def __init__(self):
+        self.c, self.f = lax.axis_index("ctx"), lax.axis_index("fsdp")
+        self.y, self.z, self.core = self.c // 4, (self.c // 2) % 2, self.c % 2
+        self.x, self.half = self.f // 2, self.f % 2
+
+    def block(self, dy, flip, other=False):
+        core = 1 - self.core if other else self.core
+        return ((self.y + dy) % 4) * 4 + (1 - self.z if flip else self.z) * 2 + core
+
+    def shard(self, dx, flip):
+        return ((self.x + dx) % 4) * 2 + (1 - self.half if flip else self.half)
+
+    def to_ctx(self, dy, flip, other=False):
+        return (self.block(dy, flip, other), self.f)
+
+    def to_fsdp(self, dx, flip):
+        return (self.c, self.shard(dx, flip))
+
+    def to_swap(self):
+        return (2 * self.f + self.c % 2, self.c // 2)
+
+
+class Post:
+    def __init__(self, place, send, recv):
+        self.place, self.send, self.recv, self.started = place, send, recv, []
+
+    def copy(self, source, target, device):
+        at = len(self.started)
+        copy = pltpu.make_async_remote_copy(
+            src_ref=source, dst_ref=target, send_sem=self.send.at[at], recv_sem=self.recv.at[at],
+            device_id=device, device_id_type=MESH,
+        )
+        self.started.append(copy)
+        copy.start()
+        return copy
+
+    def greet(self):
+        place = self.place
+        barrier = pltpu.get_barrier_semaphore()
+        partners = [
+            place.to_ctx(1, False), place.to_ctx(-1, False), place.to_ctx(0, True),
+            place.to_ctx(0, False, True), place.to_fsdp(1, False), place.to_fsdp(-1, False),
+            place.to_fsdp(0, True),
+        ]
+        for partner in partners:
+            pl.semaphore_signal(barrier, inc=1, device_id=partner, device_id_type=MESH)
+        swap = place.to_swap()
+        same = jnp.logical_and(swap[0] == place.c, swap[1] == place.f)
+
+        @pl.when(jnp.logical_not(same))
+        def _():
+            pl.semaphore_signal(barrier, inc=1, device_id=swap, device_id_type=MESH)
+
+        pl.semaphore_wait(barrier, len(partners) + jnp.where(same, 0, 1))
+
+    def close(self):
+        for copy in self.started:
+            copy.wait_send()
+
+
+def gather_ctx(post, own, buf, cut):
+    place = post.place
+    here = post.place.block(0, False)
+    crossed = []
+
+    def send(at, *to):
+        return post.copy(buf.at[at], buf.at[at], place.to_ctx(*to))
+
+    def cross(at):
+        crossed.append(post.copy(buf.at[at], buf.at[at], place.to_ctx(0, False, True)))
+
+    def first(*to):
+        return post.copy(own, buf.at[here], place.to_ctx(*to))
+
+    to_pair = first(0, True)
+    to_next, to_last = first(1, False), first(-1, False)
+    crossed.append(first(0, False, True))
+    yield
+    to_pair.wait_recv()
+    pair = place.block(0, True)
+    pair_next, pair_last = send(pair, 1, False), send(pair, -1, False)
+    cross(pair)
+    yield
+    to_next.wait_recv()
+    last = place.block(-1, False)
+    low = post.copy(
+        buf.at[last, pl.ds(0, cut)], buf.at[last, pl.ds(0, cut)], place.to_ctx(1, False)
+    )
+    cross(last)
+    to_last.wait_recv()
+    after = place.block(1, False)
+    rest = buf.shape[1] - cut
+    high = post.copy(
+        buf.at[after, pl.ds(cut, rest)], buf.at[after, pl.ds(cut, rest)], place.to_ctx(-1, False)
+    )
+    cross(after)
+    yield
+    low.wait_recv()
+    high.wait_recv()
+    far = place.block(2, False)
+    pair_far = send(far, 0, True)
+    cross(far)
+    yield
+    pair_next.wait_recv()
+    cross(place.block(-1, True))
+    pair_last.wait_recv()
+    cross(place.block(1, True))
+    yield
+    pair_far.wait_recv()
+    cross(place.block(2, True))
+    yield
+    for copy in crossed:
+        copy.wait_recv()
+
+
+def gather_fsdp(post, own, buf, cut):
+    place = post.place
+    here = place.shard(0, False)
+    rest = buf.shape[1] - cut
+
+    def whole(at, dx):
+        return post.copy(buf.at[at], buf.at[at], place.to_fsdp(dx, False))
+
+    def lower(at):
+        piece = buf.at[at, pl.ds(0, cut)]
+        return post.copy(piece, piece, place.to_fsdp(1, False))
+
+    def upper(at):
+        piece = buf.at[at, pl.ds(cut, rest)]
+        return post.copy(piece, piece, place.to_fsdp(-1, False))
+
+    to_pair = post.copy(own, buf.at[here], place.to_fsdp(0, True))
+    to_next = post.copy(own, buf.at[here], place.to_fsdp(1, False))
+    to_last = post.copy(own, buf.at[here], place.to_fsdp(-1, False))
+    yield
+    to_next.wait_recv()
+    low = lower(place.shard(-1, False))
+    to_last.wait_recv()
+    high = upper(place.shard(1, False))
+    yield
+    to_pair.wait_recv()
+    pair = place.shard(0, True)
+    pair_next, pair_last = whole(pair, 1), whole(pair, -1)
+    yield
+    pair_next.wait_recv()
+    pair_low = lower(place.shard(-1, True))
+    pair_last.wait_recv()
+    pair_high = upper(place.shard(1, True))
+    yield
+    for copy in (low, high, pair_low, pair_high):
+        copy.wait_recv()
+
+
+def add_into(target, *parts):
+    step = 16
+    rows = target.shape[0]
+
+    def body(at, carry):
+        take = pl.ds(pl.multiple_of(at * step, step), step)
+        total = parts[0][take, :].astype(F32)
+        for part in parts[1:]:
+            total = total + part[take, :].astype(F32)
+        target[take, :] = total.astype(target.dtype)
+        return carry
+
+    lax.fori_loop(0, rows // step, body, 0)
+
+
+def reduce_ctx(post, part, core, pair_in, half_in, ring_in, cross_in, last_in, total):
+    place = post.place
+    order = [(2, True), (1, True), (-1, True), (2, False), (1, False), (-1, False), (0, True), (0, False)]
+    crossed = [
+        post.copy(part.at[place.block(*to, True)], core.at[at], place.to_ctx(0, False, True))
+        for at, to in enumerate(order)
+    ]
+    cut = half_in.shape[1]
+
+    def own(at):
+        crossed[at].wait_recv()
+        return part.at[place.block(*order[at])]
+
+    yield
+    add_into(core.at[0], own(0), core.at[0])
+    far = post.copy(core.at[0], pair_in, place.to_ctx(0, True))
+    add_into(core.at[1], own(1), core.at[1])
+    cross_next = post.copy(core.at[1], cross_in.at[0], place.to_ctx(1, False))
+    add_into(core.at[2], own(2), core.at[2])
+    cross_last = post.copy(core.at[2], cross_in.at[1], place.to_ctx(-1, False))
+    for at in (3, 4, 5, 6):
+        add_into(core.at[at], own(at), core.at[at])
+    yield
+    far.wait_recv()
+    add_into(core.at[3], core.at[3], pair_in)
+    low = post.copy(core.at[3, pl.ds(0, cut)], half_in.at[0], place.to_ctx(1, False))
+    high = post.copy(core.at[3, pl.ds(cut, cut)], half_in.at[1], place.to_ctx(-1, False))
+    yield
+    cross_next.wait_recv()
+    cross_last.wait_recv()
+    add_into(core.at[6], core.at[6], cross_in.at[0], cross_in.at[1])
+    last = post.copy(core.at[6], last_in, place.to_ctx(0, True))
+    yield
+    low.wait_recv()
+    add_into(core.at[4, pl.ds(0, cut)], core.at[4, pl.ds(0, cut)], half_in.at[0])
+    ring_next = post.copy(core.at[4], ring_in.at[0], place.to_ctx(1, False))
+    high.wait_recv()
+    add_into(core.at[5, pl.ds(cut, cut)], core.at[5, pl.ds(cut, cut)], half_in.at[1])
+    ring_last = post.copy(core.at[5], ring_in.at[1], place.to_ctx(-1, False))
+    yield
+    last.wait_recv()
+    ring_next.wait_recv()
+    ring_last.wait_recv()
+    add_into(total, own(7), core.at[7], ring_in.at[0], ring_in.at[1], last_in)
+
+
+def reduce_fsdp(post, part, hold, low_in, high_in, ring_in, pair_in, total):
+    place = post.place
+    cut, rest = low_in.shape[1], high_in.shape[1]
+    lower, upper = pl.ds(0, cut), pl.ds(cut, rest)
+    halves = []
+    for side, flip in enumerate((True, False)):
+        far = place.shard(2, flip)
+        low = post.copy(part.at[far, lower], low_in.at[side], place.to_fsdp(1, False))
+        high = post.copy(part.at[far, upper], high_in.at[side], place.to_fsdp(-1, False))
+        halves.append((low, high))
+    yield
+    rings = []
+    for side, flip in enumerate((True, False)):
+        low, high = halves[side]
+        after, before = place.shard(1, flip), place.shard(-1, flip)
+        low.wait_recv()
+        add_into(hold.at[side, lower], part.at[after, lower], low_in.at[side])
+        add_into(hold.at[side, upper], part.at[after, upper])
+        to_next = post.copy(hold.at[side], ring_in.at[side, 0], place.to_fsdp(1, False))
+        high.wait_recv()
+        add_into(hold.at[2 + side, lower], part.at[before, lower])
+        add_into(hold.at[2 + side, upper], part.at[before, upper], high_in.at[side])
+        to_last = post.copy(hold.at[2 + side], ring_in.at[side, 1], place.to_fsdp(-1, False))
+        rings.append((to_next, to_last))
+        yield
+    for copy in rings[0]:
+        copy.wait_recv()
+    add_into(hold.at[4], part.at[place.shard(0, True)], ring_in.at[0, 0], ring_in.at[0, 1])
+    across = post.copy(hold.at[4], pair_in, place.to_fsdp(0, True))
+    yield
+    for copy in rings[1]:
+        copy.wait_recv()
+    across.wait_recv()
+    add_into(total, part.at[place.shard(0, False)], ring_in.at[1, 0], ring_in.at[1, 1], pair_in)
+
+
+def run(*flows):
+    flows = list(flows)
+    while flows:
+        flows = [flow for flow in flows if next(flow, flows) is not flows]
+
+
+class Swap:
+    def __init__(self, place, source, target, send, recv, local):
+        device = place.to_swap()
+        self.same = jnp.logical_and(device[0] == place.c, device[1] == place.f)
+        self.away = pltpu.make_async_remote_copy(
+            src_ref=source, dst_ref=target, send_sem=send, recv_sem=recv, device_id=device,
+            device_id_type=MESH,
+        )
+        self.stay = pltpu.make_async_copy(source, target, local)
+        pl.when(jnp.logical_not(self.same))(lambda: self.away.start())
+        pl.when(self.same)(lambda: self.stay.start())
+
+    def wait(self):
+        pl.when(jnp.logical_not(self.same))(lambda: self.away.wait())
+        pl.when(self.same)(lambda: self.stay.wait())
+
+
+def gather_kernel(
+    x_in, g_in, pos_in, in_rows, out_rows, small_in,
+    x_all, g_all, pos_all, w_in, w_out, small_all,
+    piece, send, recv, local, swap_send, swap_recv,
+):
+    place = Place()
+    post = Post(place, send, recv)
+    post.greet()
+    swap = Swap(place, out_rows, piece, swap_send, swap_recv, local.at[6])
+    here, shard = place.block(0, False), place.shard(0, False)
+    keeps = []
+    for own, buf, at in (
+        (x_in, x_all, here), (g_in, g_all, here), (pos_in, pos_all, here), (in_rows, w_in, shard),
+        (small_in, small_all, shard),
+    ):
+        keeps.append(pltpu.make_async_copy(own, buf.at[at], local.at[len(keeps)]))
+        keeps[-1].start()
+    x_flow = gather_ctx(post, x_in, x_all, x_in.shape[0] // 2)
+    in_flow = gather_fsdp(post, in_rows, w_in, in_rows.shape[0] // 2)
+    next(x_flow)
+    next(in_flow)
+    pos_flow = gather_ctx(post, pos_in, pos_all, 8)
+    next(pos_flow)
+    small_flow = gather_fsdp(post, small_in, small_all, 16)
+    next(small_flow)
+    next(x_flow)
+    swap.wait()
+    out_flow = gather_fsdp(post, piece, w_out, 48)
+    next(out_flow)
+    keeps.append(pltpu.make_async_copy(piece, w_out.at[shard], local.at[5]))
+    keeps[-1].start()
+    next(x_flow)
+    next(in_flow)
+    g_flow = gather_ctx(post, g_in, g_all, g_in.shape[0] // 2)
+    run(x_flow, in_flow, g_flow, out_flow, pos_flow, small_flow)
+    for keep in keeps:
+        keep.wait()
+    post.close()
+
+
+def gather(tokens, cotangent, positions, in_rows, out_rows, small, ctx, fsdp):
+    many = 3 * 16 + 3 * 9
+    shapes = [
+        jax.ShapeDtypeStruct((count,) + array.shape, array.dtype)
+        for count, array in (
+            (ctx, tokens), (ctx, cotangent), (ctx, positions), (fsdp, in_rows), (fsdp, out_rows),
+            (fsdp, small),
+        )
+    ]
+    whole = pl.BlockSpec(memory_space=pl.ANY)
+    return pl.pallas_call(
+        gather_kernel,
+        out_shape=tuple(shapes),
+        in_specs=[whole] * 6,
+        out_specs=(whole,) * 6,
+        scratch_shapes=[
+            pltpu.VMEM(out_rows.shape, out_rows.dtype),
+            pltpu.SemaphoreType.DMA((many,)),
+            pltpu.SemaphoreType.DMA((many,)),
+            pltpu.SemaphoreType.DMA((7,)),
+            pltpu.SemaphoreType.DMA,
+            pltpu.SemaphoreType.DMA,
+        ],
+        compiler_params=pltpu.CompilerParams(
+            collective_id=0, has_side_effects=True, vmem_limit_bytes=16 * 1024 * 1024
+        ),
+        name="gather",
+    )(tokens, cotangent, positions, in_rows, out_rows, small)
+
+
+def reduce_kernel(
+    out_part, hid_part, in_grad, out_grad, vector_in,
+    out_total, hid_total, in_all, out_all, vector_all,
+    core_a, pair_a, half_a, ring_a, cross_a, last_a,
+    core_b, pair_b, half_b, ring_b, cross_b, last_b,
+    in_hold, in_low, in_high, in_ring, in_pair, in_sum,
+    out_hold, out_low, out_high, out_ring, out_pair, out_sum, out_piece,
+    vector_shards, vector_sum,
+    send, recv, local, swap_send, swap_recv,
+):
+    place = Place()
+    post = Post(place, send, recv)
+    post.greet()
+    here, shard = place.block(0, False), place.shard(0, False)
+    keeps = []
+
+    def keep(source, target):
+        keeps.append(pltpu.make_async_copy(source, target, local.at[len(keeps)]))
+        keeps[-1].start()
+
+    def in_flow():
+        yield from reduce_fsdp(post, in_grad, in_hold, in_low, in_high, in_ring, in_pair, in_sum)
+        keep(in_sum, in_all.at[here])
+        yield from gather_ctx(post, in_sum, in_all, in_sum.shape[0] // 2)
+
+    def out_flow():
+        yield from reduce_fsdp(
+            post, out_grad, out_hold, out_low, out_high, out_ring, out_pair, out_sum
+        )
+        swap = Swap(place, out_sum, out_piece, swap_send, swap_recv, local.at[4])
+        yield
+        swap.wait()
+        keep(out_piece, out_all.at[here])
+        yield from gather_ctx(post, out_piece, out_all, 48)
+
+    def vector_flow():
+        keep(vector_in, vector_shards.at[shard])
+        mine = keeps[-1]
+        yield from gather_fsdp(post, vector_in, vector_shards, 8)
+        mine.wait()
+        total = vector_shards[0]
+        for at in range(1, vector_shards.shape[0]):
+            total = total + vector_shards[at]
+        vector_sum[...] = total
+        keep(vector_sum, vector_all.at[here])
+        yield from gather_ctx(post, vector_sum, vector_all, 8)
+
+    run(
+        in_flow(),
+        out_flow(),
+        reduce_ctx(post, out_part, core_a, pair_a, half_a, ring_a, cross_a, last_a, out_total),
+        reduce_ctx(post, hid_part, core_b, pair_b, half_b, ring_b, cross_b, last_b, hid_total),
+        vector_flow(),
+    )
+    for at, kept in enumerate(keeps):
+        if at != 0:
+            kept.wait()
+    post.close()
+
+
+def reduce(out_part, hid_part, in_grad, out_grad, vector):
+    ctx, rows, width = out_part.shape
+    whole, vmem = pl.BlockSpec(memory_space=pl.ANY), pl.BlockSpec(memory_space=pltpu.VMEM)
+
+    def low(*shape):
+        return pltpu.VMEM(shape, BF16)
+
+    def ctx_scratch():
+        return [
+            low(ctx // 2, rows, width), low(rows, width), low(2, rows // 2, width),
+            low(2, rows, width), low(2, rows, width), low(rows, width),
+        ]
+
+    def fsdp_scratch(part, cut):
+        depth, columns = part.shape[1:]
+        return [
+            low(5, depth, columns), low(2, cut, columns), low(2, depth - cut, columns),
+            low(2, 2, depth, columns), low(depth, columns), low(depth, columns),
+        ]
+
+    many = 2 * 16 + 2 * 9 + 2 * 16 + 9 + 16
+    total = jax.ShapeDtypeStruct((rows, width), F32)
+    return pl.pallas_call(
+        reduce_kernel,
+        out_shape=(
+            total,
+            total,
+            jax.ShapeDtypeStruct((ctx,) + in_grad.shape[1:], BF16),
+            jax.ShapeDtypeStruct((ctx,) + out_grad.shape[1:], BF16),
+            jax.ShapeDtypeStruct((ctx,) + vector.shape, F32),
+        ),
+        in_specs=[vmem] * 5,
+        out_specs=(vmem, vmem, whole, whole, whole),
+        scratch_shapes=ctx_scratch()
+        + ctx_scratch()
+        + fsdp_scratch(in_grad, in_grad.shape[1] // 2)
+        + fsdp_scratch(out_grad, 48)
+        + [
+            low(*out_grad.shape[1:]),
+            pltpu.VMEM((in_grad.shape[0],) + vector.shape, F32),
+            pltpu.VMEM(vector.shape, F32),
+            pltpu.SemaphoreType.DMA((many,)),
+            pltpu.SemaphoreType.DMA((many,)),
+            pltpu.SemaphoreType.DMA((5,)),
+            pltpu.SemaphoreType.DMA,
+            pltpu.SemaphoreType.DMA,
+        ],
+        compiler_params=pltpu.CompilerParams(
+            collective_id=1, has_side_effects=True, vmem_limit_bytes=60 * 1024 * 1024
+        ),
+        name="reduce",
+    )(out_part, hid_part, in_grad, out_grad, vector)
+
+
 def gelu_tanh(values):
     return (
         0.5 * values * (1.0 + jnp.tanh(GELU_COEF * (values + 0.044715 * values * values * values)))
@@ -156,7 +617,7 @@
     w_fc1, b_fc1, w_fc2, b_fc2,
 ):
     ctx, fsdp = lax.axis_size("ctx"), lax.axis_size("fsdp")
-    c, f = lax.axis_index("ctx"), lax.axis_index("fsdp")
+    c = lax.axis_index("ctx")
     share = ctx // fsdp
     rows, width = tokens.shape[1:]
     seq = rows * ctx
@@ -165,19 +626,10 @@
     own_rows = width // fsdp
     tokens = tokens.reshape(rows, width)
     cotangent = cotangent.reshape(rows, width)
-    swap = [
-        (cs * fsdp + fs, (share * fs + cs % share) * fsdp + cs // share)
-        for cs in range(ctx)
-        for fs in range(fsdp)
-    ]
-
-    small = jnp.concatenate([ln_gain, ln_bias, b_qkv, b_fc1, b_dense, b_fc2])
-    small = lax.all_gather(small, "fsdp", axis=0)
-    small_at, at = [], 0
-    for piece in (ln_gain, ln_bias, b_qkv, b_fc1, b_dense, b_fc2):
-        small_at.append(small[:, at : at + piece.shape[0]].reshape(-1).astype(F32))
-        at += piece.shape[0]
-    gain, shift, bias_qkv, bias_fc1, bias_dense, bias_fc2 = small_at
+
+    vectors = (ln_gain, ln_bias, b_dense, b_fc2, b_qkv, b_fc1)
+    small = jnp.concatenate([vector.reshape(-1, own_rows) for vector in vectors])
+    small = jnp.pad(small, ((0, 32 - small.shape[0]), (0, 0)))
     in_rows = jnp.concatenate(
         [
             lax.dynamic_slice_in_dim(w_qkv, part * width + c * own_width, own_width, 1)
@@ -186,26 +638,39 @@
         + [lax.dynamic_slice_in_dim(w_fc1, c * own_ff, own_ff, 1)],
         axis=1,
     )
-    w_in = lax.all_gather(in_rows, "fsdp", axis=0, tiled=True)
-    out_rows = jnp.concatenate(
+
+    def own_piece(weight, amount):
+        step = amount // fsdp
+        return lax.dynamic_slice_in_dim(weight, (c % share) * amount + (c // share) * step, step, 0)
+
+    out_rows = jnp.concatenate([own_piece(w_dense, own_width), own_piece(w_fc2, own_ff)])
+    dense_step, fc2_step = own_width // fsdp, own_ff // fsdp
+    pos_rows = jnp.broadcast_to(positions.reshape(1, rows), (16, rows))
+    x_all, g_all, pos_all, w_in, w_out, small_all = gather(
+        tokens, cotangent, pos_rows, in_rows, out_rows, small, ctx, fsdp
+    )
+    x_all, g_all = x_all.reshape(seq, width), g_all.reshape(seq, width)
+    w_in = w_in.reshape(width, -1)
+    w_out = jnp.concatenate(
         [
-            lax.dynamic_slice_in_dim(w_dense, lax.rem(c, share) * own_width, own_width, 0),
-            lax.dynamic_slice_in_dim(w_fc2, lax.rem(c, share) * own_ff, own_ff, 0),
-        ],
-        axis=0,
-    )
-    w_out = lax.ppermute(out_rows, ("ctx", "fsdp"), swap)
-    own_bias_qkv = jnp.concatenate(
+            w_out[:, :dense_step].reshape(own_width, width),
+            w_out[:, dense_step:].reshape(own_ff, width),
+        ]
+    )
+    small_at, at = [], 0
+    for vector in vectors:
+        count = vector.shape[0] // own_rows
+        small_at.append(small_all[:, at : at + count].reshape(-1).astype(F32))
+        at += count
+    gain, shift, bias_dense, bias_fc2, bias_qkv, bias_fc1 = small_at
+    own_bias = jnp.concatenate(
         [
             lax.dynamic_slice_in_dim(bias_qkv, part * width + c * own_width, own_width, 0)
             for part in range(3)
         ]
-    )
-    own_bias_fc1 = lax.dynamic_slice_in_dim(bias_fc1, c * own_ff, own_ff, 0)
-
-    x_all = lax.all_gather(tokens, "ctx", axis=0, tiled=True)
-    g_all = lax.all_gather(cotangent, "ctx", axis=0, tiled=True)
-    pos_all = lax.all_gather(positions.reshape(rows), "ctx", axis=0, tiled=True)
+        + [lax.dynamic_slice_in_dim(bias_fc1, c * own_ff, own_ff, 0)]
+    )
+
     x_f = x_all.astype(F32)
     mean = jnp.mean(x_f, axis=1, keepdims=True)
     centred = x_f - mean
@@ -213,10 +678,10 @@
     hidden = (centred * inverse * gain + shift).astype(BF16)
 
     cut = 3 * own_width
-    projected = jnp.dot(hidden, w_in[:, :cut], preferred_element_type=F32) + own_bias_qkv
-    up_value = jnp.dot(hidden, w_in[:, cut:], preferred_element_type=F32) + own_bias_fc1
+    projected = jnp.dot(hidden, w_in[:, :cut], preferred_element_type=F32) + own_bias[:cut]
+    up_value = jnp.dot(hidden, w_in[:, cut:], preferred_element_type=F32) + own_bias[cut:]
     activated = gelu_tanh(up_value).astype(BF16)
-    tables = turn_tables(pos_all, own_width)
+    tables = turn_tables(pos_all[:, 0].reshape(seq), own_width)
     queries = turn(projected[:, :own_width], tables, False).astype(BF16)
     keys = turn(projected[:, own_width : 2 * own_width], tables, False).astype(BF16)
     values = projected[:, 2 * own_width :].astype(BF16)
@@ -225,22 +690,6 @@
     d_act = lax.dot_general(g_all, w_out[own_width:], NT, preferred_element_type=F32)
     d_up = jax.vjp(gelu_tanh, up_value)[1](d_act)[0].astype(BF16)
 
-    def scatter(term):
-        return lax.psum_scatter(term.astype(BF16), "fsdp", scatter_dimension=0, tiled=True)
-
-    def from_ctx(piece):
-        return lax.all_gather(piece, "ctx", axis=0)
-
-    def swapped(piece):
-        return from_ctx(lax.ppermute(piece, ("ctx", "fsdp"), swap))
-
-    def rows_of(pieces, amount):
-        pieces = pieces.astype(F32).reshape(fsdp, share, amount // fsdp, width)
-        return pieces.transpose(1, 0, 2, 3).reshape(share * amount, width)
-
-    grad_fc1 = from_ctx(scatter(lax.dot_general(hidden, d_up, TN, preferred_element_type=F32)))
-    grad_fc2 = swapped(scatter(lax.dot_general(activated, g_all, TN, preferred_element_type=F32)))
-
     blocks = block_order.shape[0]
     where = jnp.argsort(block_order).astype(jnp.int32)
     attended, d_query, d_key, d_value = attention(
@@ -250,26 +699,41 @@
         [turn(d_query, tables, True), turn(d_key, tables, True), d_value], axis=1
     ).astype(BF16)
 
-    grad_qkv = from_ctx(
-        scatter(lax.dot_general(hidden, d_projected, TN, preferred_element_type=F32))
-    )
-    grad_dense = swapped(scatter(lax.dot_general(attended, g_all, TN, preferred_element_type=F32)))
-
-    branches = jnp.dot(attended, w_out[:own_width], preferred_element_type=F32) + jnp.dot(
-        activated, w_out[own_width:], preferred_element_type=F32
-    )
-    branches = lax.psum_scatter(branches.astype(BF16), "ctx", scatter_dimension=0, tiled=True)
-    x_own = tokens.astype(F32)
-    result = x_own + branches.astype(F32) + bias_dense + bias_fc2
-
-    d_hidden = lax.dot_general(
-        d_projected, w_in[:, :cut], NT, preferred_element_type=F32
-    ) + lax.dot_general(d_up, w_in[:, cut:], NT, preferred_element_type=F32)
+    inner = jnp.concatenate([d_projected, d_up], axis=1)
+    outer = jnp.concatenate([attended, activated], axis=1)
+    grad_in = lax.dot_general(hidden, inner, TN, preferred_element_type=F32).astype(BF16)
+    grad_out = lax.dot_general(outer, g_all, TN, preferred_element_type=F32).astype(BF16)
+    grad_out = jnp.concatenate(
+        [
+            grad_out[:own_width].reshape(fsdp, dense_step, width),
+            grad_out[own_width:].reshape(fsdp, fc2_step, width),
+        ],
+        axis=1,
+    )
+    branches = jnp.dot(outer, w_out, preferred_element_type=F32).astype(BF16)
+    d_hidden = lax.dot_general(inner, w_in, NT, preferred_element_type=F32)
     part_gain = jnp.sum(d_hidden * (centred * inverse), axis=0)
     part_shift = jnp.sum(d_hidden, axis=0)
-    d_hidden = lax.psum_scatter(
-        d_hidden.astype(BF16), "ctx", scatter_dimension=0, tiled=True
-    ).astype(F32)
+    columns = jnp.sum(inner.astype(F32), axis=0)
+    vector = jnp.concatenate(
+        [
+            part_gain,
+            part_shift,
+            jnp.sum(cotangent.astype(F32), axis=0),
+            columns,
+            jnp.zeros((16 * 1024 - 3 * width - columns.shape[0],), F32),
+        ]
+    ).reshape(16, 1024)
+    branches, d_hidden, in_all, out_all, vector_all = reduce(
+        branches.reshape(ctx, rows, width),
+        d_hidden.astype(BF16).reshape(ctx, rows, width),
+        grad_in.reshape(fsdp, own_rows, -1),
+        grad_out,
+        vector,
+    )
+
+    x_own = tokens.astype(F32)
+    result = x_own + branches + bias_dense + bias_fc2
     own_mean = jnp.mean(x_own, axis=1, keepdims=True)
     own_centred = x_own - own_mean
     own_inverse = lax.rsqrt(jnp.mean(own_centred * own_centred, axis=1, keepdims=True) + NORM_EPS)
@@ -281,42 +745,36 @@
         - normed * jnp.mean(scaled * normed, axis=1, keepdims=True)
     )
 
-    vector = jnp.concatenate(
-        [
-            part_gain,
-            part_shift,
-            jnp.sum(cotangent.astype(F32), axis=0),
-            jnp.sum(d_projected.astype(F32), axis=0),
-            jnp.sum(d_up.astype(F32), axis=0),
-        ]
-    )
-    vector = lax.all_gather(vector, "ctx", axis=0)
-    sums = jnp.sum(vector[:, : 3 * width], axis=0)
-    columns = vector[:, 3 * width : 3 * width + cut].reshape(ctx, 3, own_width)
+    f = lax.axis_index("fsdp")
+    vector_all = vector_all.reshape(ctx, -1)
+    sums = jnp.sum(vector_all[:, : 3 * width], axis=0).reshape(3, width)
+    sums = lax.dynamic_slice_in_dim(sums, f * own_rows, own_rows, 1)
+    columns = vector_all[:, 3 * width : 3 * width + cut].reshape(ctx, 3, own_width)
     columns = columns.transpose(1, 0, 2).reshape(3 * width)
-    units = vector[:, 3 * width + cut :].reshape(ff)
-    pieces = [sums[:width], sums[width : 2 * width], sums[2 * width :], columns, units]
-    pieces = jnp.concatenate([piece.reshape(fsdp, -1) for piece in pieces], axis=1)
-    pieces = lax.psum_scatter(pieces, "fsdp", scatter_dimension=0, tiled=True).reshape(-1)
-    cuts = [own_rows, 2 * own_rows, 3 * own_rows, 3 * own_rows + 3 * width // fsdp]
-    d_gain, d_shift, d_bias, d_bias_qkv, d_bias_fc1 = jnp.split(pieces, cuts)
-
-    out_fc1 = grad_fc1.transpose(1, 0, 2).astype(F32).reshape(own_rows, ff)
-    out_qkv = grad_qkv.reshape(ctx, own_rows, 3, own_width).transpose(1, 2, 0, 3)
+    units = vector_all[:, 3 * width + cut : 3 * width + cut + own_ff].reshape(ff)
+    d_bias_qkv = lax.dynamic_slice_in_dim(columns, f * (3 * own_rows), 3 * own_rows, 0)
+    d_bias_fc1 = lax.dynamic_slice_in_dim(units, f * (ff // fsdp), ff // fsdp, 0)
+
+    def rows_of(pieces, amount):
+        pieces = pieces.astype(F32).reshape(fsdp, share, amount // fsdp, width)
+        return pieces.transpose(1, 0, 2, 3).reshape(share * amount, width)
+
+    out_fc1 = in_all[:, :, cut:].transpose(1, 0, 2).astype(F32).reshape(own_rows, ff)
+    out_qkv = in_all[:, :, :cut].reshape(ctx, own_rows, 3, own_width).transpose(1, 2, 0, 3)
     out_qkv = out_qkv.astype(F32).reshape(own_rows, 3 * width)
     return (
         result.astype(BF16).reshape(1, rows, width),
         input_grad.reshape(1, rows, width),
-        d_gain,
-        d_shift,
+        sums[0],
+        sums[1],
         out_qkv,
         d_bias_qkv,
-        rows_of(grad_dense, own_width),
-        d_bias,
+        rows_of(out_all[:, :dense_step], own_width),
+        sums[2],
         out_fc1,
         d_bias_fc1,
-        rows_of(grad_fc2, own_ff),
-        d_bias,
+        rows_of(out_all[:, dense_step:], own_ff),
+        sums[2],
     )
 
 

time: 1110 us -> 566 us (0.51)
  waiting for transfers between devices: 634 us -> 0 us
  Pallas kernels: 36.6 us -> 303 us
  blocking collectives: 157 us -> 0 us
  local copies, waits for them, and re-layouts: 74.7 us -> 112 us
  matrix products: 114 us -> 79.3 us
  starting transfers between devices: 25.4 us -> 0 us
  other arithmetic: 43.7 us -> 60 us
  between operations: 14.9 us -> 1.53 us
    reduce_scatter x6 -> x0, waiting for transfers between devices: 390 us -> none  [the longest x4 199 us: scatter(): lax.psum_scatter(term.astype(BF16), 'fsdp', scatter_dimension=0, tiled=True)]
    pallas_call x0 -> x2, Pallas kernels: none -> 266 us  [the longest x1 161 us: reduce(): pl.pallas_call(reduce_kernel, out_shape=(total, total, jax.ShapeDtypeStru...]
    all_gather x7 -> x0, waiting for transfers between devices: 194 us -> none  [the longest x4 115 us: from_ctx(): return lax.all_gather(piece, 'ctx', axis=0)]
    all_gather x3 -> x0, blocking collectives: 157 us -> none  [the longest x1 107 us: on_device(): pos_all = lax.all_gather(positions.reshape(rows), 'ctx', axis=0, tiled=True)]
    unnamed x15 -> x0, waiting for transfers between devices: 50 us -> none
    dot_general x10 -> x6, matrix products: 96.1 us -> 59.9 us  [the longest x1 15.7 us: on_device(): d_hidden = lax.dot_general(inner, w_in, NT, preferred_element_type=F32)]
    ppermute x3 -> x0, starting transfers between devices: 24.2 us -> none  [the longest x1 21.2 us: on_device(): w_out = lax.ppermute(out_rows, ('ctx', 'fsdp'), swap)]
    unnamed x100 -> x107, local copies, waits for them, and re-layouts: 23.8 us -> 36.2 us
  transfers between devices with their start and end apart: 17 -> 0, of which waited for: 12 -> 0; matrix products, arithmetic and copies ran while one was open for 19% -> 0% of each run, Pallas kernels for 0% -> 0%
where the time goes in v2:
time: 566 us; the launch traced here: 555 us
  Pallas kernels  303 us (54%)
  local copies, waits for them, and re-layouts  112 us (20%)
  matrix products  79.3 us (14%)
  other arithmetic  60 us (11%)
    pallas_call x1, Pallas kernels, reduce(): pl.pallas_call(reduce_kernel, out_shape=(total, total, jax.ShapeDtypeStru...  161 us
    pallas_call x1, Pallas kernels, gather(): pl.pallas_call(gather_kernel, out_shape=tuple(shapes), in_specs=[whole] *...  105 us
    pallas_call x1, Pallas kernels, attention(): pl.pallas_call(functools.partial(attention_kernel, block), out_shape=(jax...  36.6 us
    unnamed x107, local copies, waits for them, and re-layouts  36.2 us
    sin x1, other arithmetic, turn_tables(): cosine, sine = (jnp.cos(turned), jnp.sin(turned))  17.5 us
    dot_general x1, matrix products, on_device(): d_hidden = lax.dot_general(inner, w_in, NT, preferred_element_type=F32)  15.7 us
    reshape x2, local copies, waits for them, and re-layouts, on_device(): out_qkv = out_qkv.astype(F32).reshape(own_rows, 3 * width)  12.8 us
    dot_general x1, matrix products, on_device(): lax.dot_general(g_all, w_out[own_width:], NT, preferred_element_type=F32)  12.5 us

profile of v2, /device:TPU:1, one launch (start us, length us, event | category | flops | bytes accessed | tf_op | source)
XLA Modules:
  0.0 555.4 jit_solution(16292931619171654879)
XLA Ops:
  0.7 1.1 constant_dynamic-slice_fusion.1
  10.9 104.8 %gather.1 = (bf16[16,128,2048]{2,1,0:T(8,128)(2,1)S(1)}, bf16[16,128,2048]{2,1,0:T(8,128)(2,1)S(1)}, s32[16,16,128]{2,1,0:T(8,128)S(1)}, bf16[8,256,896]{2,1,0:T...) custom-call(bf16[128,2048]{1,0:T(8,128)(2,1)S(1)} %bitcast.81, ...), custom_call_target="tpu_custom_call" | custom-call | tf_op jit(solution)/shard_map/gather/pallas_call | solution.py:454
  115.7 3.4 copy-done.2
  119.8 3.3 copy-done.14
  123.0 1.8 copy-done.15
  125.0 4.7 convert_reduce_fusion
  129.7 1.1 copy-done.3
  130.8 2.4 multiply_reduce_fusion.1
  133.8 3.7 add_convert_fusion
  137.5 7.3 %convolution_add_fusion = f32[2048,384]{1,0:T(8,128)S(1)} fusion(bf16[2048,2048]{1,0:T(8,128)(2,1)S(1)} %add_convert_fusion, bf16[2048,896]{1,0:T(8,128)(2,1)} %bitcast.86, f32[384]{0:T(512)S(1)} %pad_maximum_fusion.7), kind=kOutput, calls=%fused_computation.25 | convolution fusion | flops 3222011904 | bytes 13108736 | tf_op jit(solution)/shard_map/dot_general | solution.py:681
  144.8 2.9 fusion.44
  147.7 2.6 fusion.45
  151.2 17.5 %multiply_sine_fusion = (f32[2048,16]{1,0:T(8,128)}, f32[2048,16]{1,0:T(8,128)}, f32[2048,16]{1,0:T(8,128)}) fusion(f32[2048]{0:T(1024)S(1)} %bitcast.118, f32[16]{0:T(128)S(1)} %negate_power_fusion), kind=kLoop, calls=%fused_computation.39 | loop fusion | flops 65536 | bytes 401472 | tf_op jit(solution)/shard_map/sin | solution.py:598
  169.7 1.1 broadcast_in_dim.13
  170.9 5.5 concatenate.71
  176.4 5.5 concatenate.73
  183.0 5.8 %concatenate.69 = f32[2048,128]{1,0:T(8,128)} concatenate(f32[2048,16]{1,0:T(8,128)} %get-tuple-element.124, f32[2048,16]{1,0:T(8,128)} %get-tuple-element.124, f32[2048,32]{1,0:T(8,128)} %add.173, f32[2048,16]{1,0:T(8,128)} %get-tuple-element.124, f32[2048,16]{1,0:T(8,128)} %get-tuple-element.124, f32[2048,32]{1,0:T(8,128)} %add.173), dimensions={1} | concatenate | bytes 2097152 | tf_op jit(solution)/shard_map/concatenate | solution.py:602
  188.7 6.9 %fusion.26 = (bf16[2048,128]{1,0:T(8,128)(2,1)S(1)}, bf16[2048,128]{1,0:T(8,128)(2,1)}) fusion(f32[2048,128]{1,0:T(8,128)} %concatenate.69, f32[2048,384]{1,0:T(8,128)} %copy-done.17, f32[2048,128]{1,0:T(8,128)} %concatenate.71, f32[2048,16]{1,0:T(8,128)} %get-tuple-element.92, f32[2048,112]{1,0:T(8,128)} %get-tuple-element.96, f32[2048,128]{1,0:T(8,128)} %concatenate.73, ...), kind=kLoop, calls=%fused_computation.58 | loop fusion | flops 4194304 | bytes 10485760 | tf_op jit(solution)/shard_map/convert_element_type | solution.py:686
  195.6 2.1 slice.226.v_in
  197.7 6.8 %convolution_convert_fusion.3.g_in = bf16[2048,128]{1,0:T(8,128)(2,1)} fusion(bf16[2048,2048]{1,0:T(8,128)(2,1)} %bitcast.83, bf16[128,2048]{1,0:T(8,128)(2,1)S(1)} %bitcast.109), kind=kOutput, calls=%fused_computation.31 | convolution fusion | flops 1074003968 | bytes 9437184 | tf_op jit(solution)/shard_map/dot_general | solution.py:688
  204.6 1.6 sort.17
  209.3 36.6 %shard_map.229 = (bf16[2048,128]{1,0:T(8,128)(2,1)S(1)}, f32[2048,128]{1,0:T(8,128)S(1)}, f32[2048,128]{1,0:T(8,128)S(1)}, f32[2048,128]{1,0:T(8,128)S(1)}) custom-call(s32[32]{0:T(128)S(1)} %get-tuple-element.28.where, bf16[2048,128]{1,0:T(8,128)(2,1)S(1)} %copy-done.9, bf16[2048,128]{1,0:T(8,128)(2,1)S(1)} %get-tuple-element.85.k_in, ...), custom_call_target="tpu_custom_call" | custom-call | flops 3221225472 | bytes 5767168 | tf_op jit(solution)/shard_map/pallas_call | solution.py:110
  248.5 2.1 fusion.33
  250.6 2.1 copy.61
  252.7 1.0 copy.62
  253.7 1.3 convert.33
  256.0 7.6 %fusion.10 = f32[2048,512]{0,1:T(8,128)S(1)} fusion(bf16[2048,2048]{1,0:T(8,128)(2,1)} %copy-done.21, bf16[2048,896]{1,0:T(8,128)(2,1)} %bitcast.87), kind=kOutput, calls=%fused_computation.32 | convolution fusion | flops 4294967296 | bytes 14680064 | tf_op jit(solution)/shard_map/dot_general | solution.py:682
  264.0 12.5 %fusion.4 = (bf16[2048,512]{0,1:T(8,128)(2,1)S(1)}, bf16[2048,512]{0,1:T(8,128)(2,1)}) fusion(f32[2048,512]{0,1:T(8,128)S(1)} %fusion.10, f32[512]{0:T(512)S(1)} %dynamic_slice.48, bf16[2048,2048]{1,0:T(8,128)(2,1)} %bitcast.84, bf16[512,2048]{1,0:T(8,128)(2,1)S(1)} %bitcast.106), kind=kOutput, calls=%fused_computation.17 | convolution fusion | flops 4323278848 | bytes 18876416 | tf_op jit(solution)/shard_map/dot_general | solution.py:690
  276.5 1.3 copy-done.25
  278.5 15.7 %fusion.43 = (f32[2048]{0:T(1024)S(1)}, f32[2048]{0:T(1024)S(1)}, bf16[2048,2048]{1,0:T(8,128)(2,1)}) fusion(f32[2048]{0:T(1024)S(1)} %rsqrt_bitcast_fusion, f32[2048]{0:T(1024)S(1)} %get-tuple-element.125, bf16[16,128,2048]{2,1,0:T(8,128)(2,1)S(1)} %bitcast.80, bf16[2048,896]{1,0:T(8,128)(2,1)} %bitcast.88, bf16[2048,512]{0,1:T(8,128)(2,1)} %copy-done.25, ...), kind=kOutput, calls=%fused_computation.116 | convolution fusion | flops 7560228864 | bytes 24150016 | tf_op jit(solution)/shard_map/dot_general | solution.py:714
  295.2 10.0 %convolution_convert_fusion.2 = bf16[640,2048]{1,0:T(8,128)(2,1)S(1)} fusion(bf16[2048,2048]{1,0:T(8,128)(2,1)} %bitcast.85, bf16[2048,512]{0,1:T(8,128)(2,1)} %get-tuple-element.88, bf16[2048,128]{0,1:T(8,128)(2,1)S(1)} %copy.60), kind=kOutput, calls=%fused_computation.23 | convolution fusion | flops 5375262720 | bytes 13631488 | tf_op jit(solution)/shard_map/dot_general | solution.py:705
  305.6 1.7 pad_maximum_fusion.2.out_grad
  308.4 10.3 %convolution_convert_fusion.1 = bf16[2048,896]{1,0:T(8,128)(2,1)} fusion(bf16[2048,2048]{1,0:T(8,128)(2,1)S(1)} %bitcast.94, bf16[2048,512]{0,1:T(8,128)(2,1)S(1)} %copy-done.26, bf16[2048,128]{0,1:T(8,128)(2,1)S(1)} %copy-done.32, bf16[2048,128]{0,1:T(8,128)(2,1)S(1)} %copy-done.30, bf16[2048,128]{0,1:T(8,128)(2,1)S(1)} %copy-done.28), kind=kOutput, calls=%fused_computation.22 | convolution fusion | flops 7532707840 | bytes 15728640 | tf_op jit(solution)/shard_map/dot_general | solution.py:704
  318.8 9.0 %convolution_convert_fusion = bf16[2048,2048]{1,0:T(8,128)(2,1)} fusion(bf16[512,2048]{1,0:T(8,128)(2,1)S(1)} %bitcast.107, bf16[128,2048]{1,0:T(8,128)(2,1)S(1)} %bitcast.110, bf16[2048,512]{0,1:T(8,128)(2,1)S(1)} %copy-done.43, bf16[2048,128]{0,1:T(8,128)(2,1)S(1)} %copy.60), kind=kOutput, calls=%fused_computation.8 | convolution fusion | flops 5383389184 | bytes 13631488 | tf_op jit(solution)/shard_map/dot_general | solution.py:713
  327.7 161.3 %reduce.3 = (f32[128,2048]{1,0:T(8,128)}, f32[128,2048]{1,0:T(8,128)}, bf16[16,256,896]{2,1,0:T(8,128)(2,1)}, bf16[16,80,2048]{2,1,0:T(8,128)(2,1)}, f32[16,16,1024]{2,1,0:T(8,128)}) custom-call(bf16[16,128,2048]{2,1,0:T(8,128)(2,1)} %bitcast.98, bf16[16,128,2048]{2,1,0:T(8,128)(2,1)} %bitcast.97, bf16[8,256,896]{2,1,0:T(8,128)(2,1)} %bitcast.100, ...), custom_call_target="tpu_custom_call" | custom-call | tf_op jit(solution)/shard_map/reduce/pallas_call | solution.py:556
  489.1 5.3 slice_convert_fusion
  494.3 6.6 %copy.64 = f32[16,256,384]{1,2,0:T(8,128)} copy(f32[16,256,384]{2,1,0:T(8,128)} %slice_convert_fusion) | data formatting | bytes 12582912 | tf_op jit(solution)/shard_map/reshape | solution.py:764
  500.9 6.2 %copy.65 = f32[256,3,16,128]{0,3,2,1:T(8,128)} copy(f32[256,3,16,128]{0,3,1,2:T(8,128)} %bitcast.90) | data formatting | bytes 12582912 | tf_op jit(solution)/shard_map/reshape | solution.py:764
  507.1 6.6 %copy.70 = f32[256,6144]{1,0:T(8,128)} copy(f32[256,6144]{0,1:T(8,128)} %bitcast.91) | data formatting | bytes 12582912
  513.7 6.7 %convert_bitcast_fusion.1 = f32[256,16,512]{2,0,1:T(8,128)} fusion(bf16[16,256,896]{2,1,0:T(8,128)(2,1)} %get-tuple-element.42), kind=kLoop, calls=%fused_computation.7 | loop fusion | flops 2097152 | bytes 12582912 | tf_op jit(solution)/shard_map/reshape | solution.py:762
  520.4 9.3 %copy.68 = f32[256,16,512]{0,2,1:T(8,128)} copy(f32[256,16,512]{2,0,1:T(8,128)} %convert_bitcast_fusion.1) | data formatting | bytes 16777216 | tf_op jit(solution)/shard_map/reshape | solution.py:762
  529.7 8.9 %copy.71 = f32[256,8192]{1,0:T(8,128)} copy(f32[256,8192]{0,1:T(8,128)} %bitcast.89) | data formatting | bytes 16777216
  538.6 2.5 slice.181
  541.1 1.1 convert_bitcast_fusion
  542.2 4.0 copy.69
  546.2 1.3 slice.177
  547.8 1.5 copy.67
  550.1 1.8 fusion.21
  (158 shorter events, 27.9 us)
Async XLA Ops:
  0.6 1.3 copy-start
  8.8 1.0 copy-start.4
  9.8 1.0 copy-start.6
  115.7 3.4 copy-start.2
  119.1 0.7 copy-start.13
  119.8 3.3 copy-start.14
  123.0 1.8 copy-start.15
  125.0 5.8 %copy-start.3 = (bf16[16,128,2048]{2,1,0:T(8,128)(2,1)S(1)}, bf16[16,128,2048]{2,1,0:T(8,128)(2,1)}, u32[]{:S(2)}) copy-start(bf16[16,128,2048]{2,1,0:T(8,128)(2,1)} %copy-done.2) | copy-start | bytes 25165828
  133.8 3.7 copy-start.37
  137.5 7.3 %copy-start.21 = (bf16[2048,2048]{1,0:T(8,128)(2,1)}, bf16[2048,2048]{1,0:T(8,128)(2,1)S(1)}, u32[]{:S(2)}) copy-start(bf16[2048,2048]{1,0:T(8,128)(2,1)S(1)} %add_convert_fusion) | copy-start | bytes 25165828
  144.8 2.9 copy-start.17
  197.7 6.8 %copy-start.35 = (bf16[8,16,2048]{2,1,0:T(8,128)(2,1)}, bf16[8,16,2048]{2,1,0:T(8,128)(2,1)S(1)}, u32[]{:S(2)}) copy-start(bf16[8,16,2048]{2,1,0:T(8,128)(2,1)S(1)} %slice.156) | copy-start | bytes 1572868
  197.7 6.8 %copy-start.42 = (s32[32]{0:T(128)S(1)}, s32[32]{0:T(128)}, u32[]{:S(2)}) copy-start(s32[32]{0:T(128)} %param.16) | copy-start | bytes 388
  206.2 1.0 copy-start.9
  207.2 1.0 copy-start.12
  208.3 1.0 copy-start.16
  245.9 0.8 copy-start.10
  245.9 4.7 copy-start.8
  246.7 1.2 copy-start.18
  246.7 1.5 copy-start.19
  246.7 1.9 copy-start.20
  263.6 14.8 %slice-start = ((s8[8388608]{0:T(1024)(128)(4,1)}), s8[4194304]{0:T(1024)(128)(4,1)S(1)}, s32[]{:S(2)}) async-start(s8[8388608]{0:T(1024)(128)(4,1)} %bitcast.79), calls=%async_computation | async-start | bytes 8388608
  263.8 12.7 %copy-start.23 = (bf16[8,64,2048]{2,1,0:T(8,128)(2,1)}, bf16[8,64,2048]{2,1,0:T(8,128)(2,1)S(1)}, u32[]{:S(2)}) copy-start(bf16[8,64,2048]{2,1,0:T(8,128)(2,1)S(1)} %slice.159) | copy-start | bytes 6291460
  263.9 13.9 %copy-start.27 = (bf16[2048,128]{0,1:T(8,128)(2,1)S(1)}, bf16[2048,128]{0,1:T(8,128)(2,1)}, u32[]{:S(2)}) copy-start(bf16[2048,128]{0,1:T(8,128)(2,1)} %copy.61) | copy-start | bytes 1572868
  263.9 13.9 %copy-start.29 = (bf16[2048,128]{0,1:T(8,128)(2,1)S(1)}, bf16[2048,128]{0,1:T(8,128)(2,1)}, u32[]{:S(2)}) copy-start(bf16[2048,128]{0,1:T(8,128)(2,1)} %copy.62) | copy-start | bytes 1572868
  263.9 13.9 %copy-start.31 = (bf16[2048,128]{0,1:T(8,128)(2,1)S(1)}, bf16[2048,128]{0,1:T(8,128)(2,1)}, u32[]{:S(2)}) copy-start(bf16[2048,128]{0,1:T(8,128)(2,1)} %copy.63) | copy-start | bytes 1572868
  263.9 14.5 %slice-start.1 = ((s8[8388608]{0:T(1024)(128)(4,1)}), s8[4194304]{0:T(1024)(128)(4,1)S(1)}, s32[]{:S(2)}) async-start(s8[8388608]{0:T(1024)(128)(4,1)} %bitcast.79), calls=%async_computation.1 | async-start | bytes 8388608
  276.5 1.3 copy-start.25
  278.5 15.7 %copy-start.7 = (bf16[1,128,2048]{2,1,0:T(8,128)(2,1)S(1)}, bf16[1,128,2048]{2,1,0:T(8,128)(2,1)}, u32[]{:S(2)}) copy-start(bf16[1,128,2048]{2,1,0:T(8,128)(2,1)} %param.15) | copy-start | bytes 1572868
  278.5 16.5 %copy-start.11 = (bf16[2048,128]{1,0:T(8,128)(2,1)S(1)}, bf16[2048,128]{1,0:T(8,128)(2,1)}, u32[]{:S(2)}) copy-start(bf16[2048,128]{1,0:T(8,128)(2,1)} %copy-done.10) | copy-start | bytes 1572868
  295.2 12.1 %slice-start.2 = ((s8[8388608]{0:T(1024)(128)(4,1)}), s8[4194304]{0:T(1024)(128)(4,1)S(1)}, s32[]{:S(2)}) async-start(s8[8388608]{0:T(1024)(128)(4,1)} %bitcast.93), calls=%async_computation.2 | async-start | bytes 8388608
  295.2 12.1 %slice-start.3 = ((s8[8388608]{0:T(1024)(128)(4,1)}), s8[4194304]{0:T(1024)(128)(4,1)S(1)}, s32[]{:S(2)}) async-start(s8[8388608]{0:T(1024)(128)(4,1)} %bitcast.93), calls=%async_computation.3 | async-start | bytes 8388608
  305.5 2.5 copy-start.26
  305.5 2.6 copy-start.28
  305.5 2.8 copy-start.30
  305.5 2.9 copy-start.32
  308.4 10.3 %copy-start.24 = (bf16[8,64,2048]{2,1,0:T(8,128)(2,1)S(1)}, bf16[8,64,2048]{2,1,0:T(8,128)(2,1)}, u32[]{:S(2)}) copy-start(bf16[8,64,2048]{2,1,0:T(8,128)(2,1)} %copy-done.23) | copy-start | bytes 6291460
  308.4 10.3 %copy-start.36 = (bf16[8,16,2048]{2,1,0:T(8,128)(2,1)S(1)}, bf16[8,16,2048]{2,1,0:T(8,128)(2,1)}, u32[]{:S(2)}) copy-start(bf16[8,16,2048]{2,1,0:T(8,128)(2,1)} %copy-done.35) | copy-start | bytes 1572868
  308.4 10.3 %copy-start.43 = (bf16[2048,512]{0,1:T(8,128)(2,1)S(1)}, bf16[2048,512]{0,1:T(8,128)(2,1)}, u32[]{:S(2)}) copy-start(bf16[2048,512]{0,1:T(8,128)(2,1)} %get-tuple-element.88) | copy-start | bytes 6291460
  547.5 1.8 copy-start.5
  547.5 2.2 copy-start.22
  547.5 2.2 copy-start.38
  547.7 2.4 copy-start.34
  547.7 2.4 copy-start.39
  547.7 2.4 copy-start.40
  549.2 2.7 copy-start.33
  549.7 5.5 copy-start.1
  554.6 0.6 copy-start.41

commit v3 on v1

v3 whole, which is shorter than its diff:
```python
import functools

import jax
import jax.numpy as jnp
import numpy as np
from jax import lax
from jax.experimental import pallas as pl
from jax.experimental.pallas import tpu as pltpu
from jax.sharding import PartitionSpec as P

HEAD_DIM = 64
ROTARY = 32
NORM_EPS = 1e-05
ROPE_BASE = 10000.0
GELU_COEF = 0.7978845608028654
F32 = jnp.float32
BF16 = jnp.bfloat16
STRIP = 256
NT = (((1,), (1,)), ((), ()))
TN = (((0,), (0,)), ((), ()))
MESH = pl.DeviceIdType.MESH
MIB = 1024 * 1024


def nt_dot(left, right):
    return lax.dot_general(left, right, NT, preferred_element_type=F32)


def tn_dot(left, right):
    return lax.dot_general(left, right, TN, preferred_element_type=F32)


def dot(left, right):
    return jnp.dot(left, right, preferred_element_type=F32)


def turn_rows(positions, width):
    half = ROTARY // 2
    frequency = ROPE_BASE ** (-(jnp.arange(half, dtype=F32) * (2.0 / ROTARY)))
    turned = positions.astype(F32)[:, None] * frequency
    both = jnp.concatenate([jnp.cos(turned), jnp.sin(turned)], axis=1)
    coarse = both.astype(BF16)
    fine = (both - coarse.astype(F32)).astype(BF16)
    rows = positions.shape[0]
    used = 4 * half + 1
    return jnp.concatenate(
        [coarse, fine, jnp.ones((rows, 1), BF16), jnp.zeros((rows, width - used), BF16)], axis=1
    )


def turn_spread(width):
    half = ROTARY // 2
    table = np.zeros((width, 3 * width), np.float32)
    for column in range(width):
        at = column % HEAD_DIM
        if at >= ROTARY:
            table[4 * half, column] = 1.0
            continue
        for part in (0, 2 * half):
            table[part + at % half, column] = 1.0
            if at < half:
                table[part + half + at, width + column] = -1.0
            else:
                table[part + half + at - half, 2 * width + column] = 1.0
    return jnp.asarray(table, BF16)


def turn(values, tables, back):
    width = values.shape[1]
    half = ROTARY // 2
    same, after, before = (tables[:, at * width : (at + 1) * width] for at in range(3))
    moved = pltpu.roll(values, width - half, 1) * after + pltpu.roll(values, half, 1) * before
    return values * same - moved if back else values * same + moved


class Place:
    def __init__(self):
        self.c, self.f = lax.axis_index("ctx"), lax.axis_index("fsdp")
        self.y, self.z, self.core = self.c // 4, (self.c // 2) % 2, self.c % 2
        self.x, self.half = self.f // 2, self.f % 2

    def block(self, dy, flip, other=False):
        core = 1 - self.core if other else self.core
        return ((self.y + dy) % 4) * 4 + (1 - self.z if flip else self.z) * 2 + core

    def shard(self, dx, flip):
        return ((self.x + dx) % 4) * 2 + (1 - self.half if flip else self.half)

    def to_ctx(self, dy, flip, other=False):
        return (self.block(dy, flip, other), self.f)

    def to_fsdp(self, dx, flip):
        return (self.c, self.shard(dx, flip))

    def to_swap(self):
        return (2 * self.f + self.c % 2, self.c // 2)


class Post:
    def __init__(self, place, send, recv):
        self.place, self.send, self.recv, self.started = place, send, recv, []
        self.left = set()

    def copy(self, source, target, device):
        at = len(self.started)
        copy = pltpu.make_async_remote_copy(
            src_ref=source, dst_ref=target, send_sem=self.send.at[at], recv_sem=self.recv.at[at],
            device_id=device, device_id_type=MESH,
        )
        self.started.append(copy)
        copy.start()
        return copy

    def greet(self):
        place = self.place
        barrier = pltpu.get_barrier_semaphore()
        partners = [
            place.to_ctx(1, False), place.to_ctx(-1, False), place.to_ctx(0, True),
            place.to_ctx(0, False, True), place.to_fsdp(1, False), place.to_fsdp(-1, False),
            place.to_fsdp(0, True),
        ]
        for partner in partners:
            pl.semaphore_signal(barrier, inc=1, device_id=partner, device_id_type=MESH)
        swap = place.to_swap()
        same = jnp.logical_and(swap[0] == place.c, swap[1] == place.f)

        @pl.when(jnp.logical_not(same))
        def _():
            pl.semaphore_signal(barrier, inc=1, device_id=swap, device_id_type=MESH)

        pl.semaphore_wait(barrier, len(partners) + jnp.where(same, 0, 1))

    def has_left(self, copy):
        copy.wait_send()
        self.left.add(id(copy))

    def close(self):
        for copy in self.started:
            if id(copy) not in self.left:
                copy.wait_send()


def gather_ctx(post, own, buf, cut):
    place = post.place
    here = post.place.block(0, False)
    crossed = []

    def send(at, *to):
        return post.copy(buf.at[at], buf.at[at], place.to_ctx(*to))

    def cross(at):
        crossed.append(post.copy(buf.at[at], buf.at[at], place.to_ctx(0, False, True)))

    def first(*to):
        return post.copy(own, buf.at[here], place.to_ctx(*to))

    to_pair = first(0, True)
    to_next, to_last = first(1, False), first(-1, False)
    crossed.append(first(0, False, True))
    yield
    to_pair.wait_recv()
    pair = place.block(0, True)
    pair_next, pair_last = send(pair, 1, False), send(pair, -1, False)
    cross(pair)
    yield
    to_next.wait_recv()
    last = place.block(-1, False)
    low = post.copy(
        buf.at[last, pl.ds(0, cut)], buf.at[last, pl.ds(0, cut)], place.to_ctx(1, False)
    )
    cross(last)
    to_last.wait_recv()
    after = place.block(1, False)
    rest = buf.shape[1] - cut
    high = post.copy(
        buf.at[after, pl.ds(cut, rest)], buf.at[after, pl.ds(cut, rest)], place.to_ctx(-1, False)
    )
    cross(after)
    yield
    low.wait_recv()
    high.wait_recv()
    far = place.block(2, False)
    pair_far = send(far, 0, True)
    cross(far)
    yield
    pair_next.wait_recv()
    cross(place.block(-1, True))
    pair_last.wait_recv()
    cross(place.block(1, True))
    yield
    pair_far.wait_recv()
    cross(place.block(2, True))
    yield
    for copy in crossed:
        copy.wait_recv()


def gather_fsdp(post, own, buf, cut):
    place = post.place
    here = place.shard(0, False)
    rest = buf.shape[1] - cut

    def whole(at, dx):
        return post.copy(buf.at[at], buf.at[at], place.to_fsdp(dx, False))

    def lower(at):
        piece = buf.at[at, pl.ds(0, cut)]
        return post.copy(piece, piece, place.to_fsdp(1, False))

    def upper(at):
        piece = buf.at[at, pl.ds(cut, rest)]
        return post.copy(piece, piece, place.to_fsdp(-1, False))

    to_pair = post.copy(own, buf.at[here], place.to_fsdp(0, True))
    to_next = post.copy(own, buf.at[here], place.to_fsdp(1, False))
    to_last = post.copy(own, buf.at[here], place.to_fsdp(-1, False))
    yield
    to_next.wait_recv()
    low = lower(place.shard(-1, False))
    to_last.wait_recv()
    high = upper(place.shard(1, False))
    yield
    to_pair.wait_recv()
    pair = place.shard(0, True)
    pair_next, pair_last = whole(pair, 1), whole(pair, -1)
    yield
    pair_next.wait_recv()
    pair_low = lower(place.shard(-1, True))
    pair_last.wait_recv()
    pair_high = upper(place.shard(1, True))
    yield
    for copy in (low, high, pair_low, pair_high):
        copy.wait_recv()


class Swap:
    def __init__(self, place, source, target, send, recv, local):
        device = place.to_swap()
        self.same = jnp.logical_and(device[0] == place.c, device[1] == place.f)
        self.away = pltpu.make_async_remote_copy(
            src_ref=source, dst_ref=target, send_sem=send, recv_sem=recv, device_id=device,
            device_id_type=MESH,
        )
        self.stay = pltpu.make_async_copy(source, target, local)
        pl.when(jnp.logical_not(self.same))(lambda: self.away.start())
        pl.when(self.same)(lambda: self.stay.start())

    def wait(self):
        pl.when(jnp.logical_not(self.same))(lambda: self.away.wait())
        pl.when(self.same)(lambda: self.stay.wait())


def first_kernel(
    x_in, g_in, turn_in, in_rows, out_rows, small_in, spread,
    x_out, g_out, hid_out, stat, q_out, k_out, v_out, d_att, act, d_up, w_in_out, w_out, turn_out,
    small_out,
    x_all, g_all, hidden, turns, w_in, pieces, piece, small_all, tables, proj, slope, vec, bias,
    send, recv, local, swap_send, swap_recv,
):
    place = Place()
    post = Post(place, send, recv)
    post.greet()
    swap = Swap(place, out_rows, piece, swap_send, swap_recv, local.at[0])
    rows, width = x_in.shape
    own_width = q_out.shape[1]
    cut = 3 * own_width
    here, shard = place.block(0, False), place.shard(0, False)
    keeps = []

    def keep(source, target):
        copy = pltpu.make_async_copy(source, target, local.at[1 + len(keeps)])
        keeps.append(copy)
        copy.start()
        return copy

    own = [
        keep(x_in, x_all.at[here]), keep(in_rows, w_in.at[shard]), keep(turn_in, turns.at[here]),
        keep(small_in, small_all.at[shard]), keep(g_in, g_all.at[here]),
    ]
    x_flow = gather_ctx(post, x_in, x_all, rows // 2)
    in_flow = gather_fsdp(post, in_rows, w_in, in_rows.shape[0] // 2)
    small_flow = gather_fsdp(post, small_in, small_all, 16)
    turn_flow = gather_ctx(post, turn_in, turns, rows // 2)
    next(x_flow)
    next(small_flow)
    next(in_flow)
    next(turn_flow)
    next(x_flow)
    swap.wait()
    keep(piece, pieces.at[shard])
    out_flow = gather_fsdp(post, piece, pieces, 48)
    next(out_flow)
    next(x_flow)
    next(in_flow)
    for _ in small_flow:
        pass
    for copy in own[:4]:
        copy.wait()

    side = small_all.shape[2]
    small_out[...] = small_all[...].astype(F32)
    for at in range(small_all.shape[0]):
        vec[0:2, at * side : (at + 1) * side] = small_out[at, 0:2, :]
    for part in range(3):
        first = part * width + place.c * own_width
        count = 3 * side
        row = small_out[first // count, pl.ds(4 + (first % count) // side, 1), :]
        bias[0:1, part * own_width : (part + 1) * own_width] = jnp.where(
            first % side == 0, row[:, :own_width], row[:, own_width:]
        )
    for part in range(2):
        row = small_out[place.c // 2, pl.ds(7 + 2 * (place.c % 2) + part, 1), :]
        bias[0:1, cut + part * side : cut + (part + 1) * side] = row

    def normalise(block):
        step = 32
        lane = lax.broadcasted_iota(jnp.int32, (step, stat.shape[1]), 1)

        def body(at, carry):
            source = pl.ds(pl.multiple_of(at * step, step), step)
            target = pl.ds(pl.multiple_of(block * rows + at * step, step), step)
            value = x_all[block, source, :].astype(F32)
            mean = jnp.mean(value, axis=1, keepdims=True)
            centred = value - mean
            inverse = lax.rsqrt(jnp.mean(centred * centred, axis=1, keepdims=True) + NORM_EPS)
            hidden[target, :] = (centred * inverse * vec[0:1, :] + vec[1:2, :]).astype(BF16)
            stat[target, :] = jnp.where(lane < HEAD_DIM, mean, inverse)
            return carry

        lax.fori_loop(0, rows // step, body, 0)

    near = [(0, False), (0, True), (1, False), (-1, False)]
    far = [(2, False), (1, True), (-1, True), (2, True)]
    next(x_flow)
    next(in_flow)
    g_flow = gather_ctx(post, g_in, g_all, rows // 2)
    next(g_flow)
    for to in near:
        normalise(place.block(*to))
    next(x_flow)
    next(in_flow)
    next(x_flow)
    for to in far[:2]:
        normalise(place.block(*to))
    next(g_flow)
    for to in far[2:]:
        normalise(place.block(*to))
    next(out_flow)
    for _ in x_flow:
        pass
    keep(x_all, x_out)
    lax.fori_loop(
        0, x_all.shape[0] // 2, lambda at, carry: normalise(2 * at + 1 - place.core) or carry, 0
    )
    keep(hidden, hid_out)
    for _ in in_flow:
        pass
    next(g_flow)
    next(out_flow)
    for _ in turn_flow:
        pass
    keep(w_in, w_in_out)
    keep(turns, turn_out)

    chunk_rows = proj.shape[0]
    step = 64
    group = chunk_rows // rows

    def project(chunk, carry):
        take = pl.ds(pl.multiple_of(chunk * chunk_rows, chunk_rows), chunk_rows)
        weight = w_in[...].reshape(width, proj.shape[1])
        proj[...] = dot(hidden[take, :], weight)
        turned = turns[pl.ds(chunk * group, group)].reshape(chunk_rows, own_width)
        tables[...] = dot(turned, spread[...])

        def body(at, inner):
            source = pl.ds(pl.multiple_of(at * step, step), step)
            target = pl.ds(pl.multiple_of(chunk * chunk_rows + at * step, step), step)
            value = proj[source, :] + bias[0:1, :]
            table = tables[source, :]
            q_out[target, :] = turn(value[:, :own_width], table, False).astype(BF16)
            k_out[target, :] = turn(value[:, own_width : 2 * own_width], table, False).astype(BF16)
            v_out[target, :] = value[:, 2 * own_width : cut].astype(BF16)
            up = value[:, cut:]
            square = up * up
            curve = jnp.tanh(GELU_COEF * up * (1.0 + 0.044715 * square))
            act[target, :] = (0.5 * up * (1.0 + curve)).astype(BF16)
            slope[target, :] = 0.5 * (1.0 + curve) + 0.5 * up * (1.0 - curve * curve) * (
                GELU_COEF * (1.0 + 3.0 * 0.044715 * square)
            )
            return inner

        lax.fori_loop(0, chunk_rows // step, body, 0)
        return carry

    chunks = hidden.shape[0] // chunk_rows
    lax.fori_loop(0, chunks // 2, project, 0)
    next(g_flow)
    next(out_flow)
    next(g_flow)
    lax.fori_loop(chunks // 2, chunks, project, 0)
    next(g_flow)
    for _ in out_flow:
        pass
    keeps[5].wait()
    dense_step = own_width // pieces.shape[0]
    fc2_step = pieces.shape[1] - dense_step
    for at in range(pieces.shape[0]):
        w_out[at * dense_step : (at + 1) * dense_step, :] = pieces[at, :dense_step, :]
        first = own_width + at * fc2_step
        w_out[first : first + fc2_step, :] = pieces[at, dense_step:, :]
    for _ in g_flow:
        pass
    own[4].wait()
    keep(g_all, g_out)

    def back(chunk, carry):
        grads = g_all[pl.ds(chunk * group, group)].reshape(chunk_rows, width)
        proj[:, : w_out.shape[0]] = nt_dot(grads, w_out[...])

        def body(at, inner):
            source = pl.ds(pl.multiple_of(at * step, step), step)
            target = pl.ds(pl.multiple_of(chunk * chunk_rows + at * step, step), step)
            d_att[target, :] = proj[source, :own_width].astype(BF16)
            d_act = proj[source, own_width : w_out.shape[0]]
            d_up[target, :] = (d_act * slope[target, :]).astype(BF16)
            return inner

        lax.fori_loop(0, chunk_rows // step, body, 0)
        return carry

    lax.fori_loop(0, chunks, back, 0)
    for copy in keeps[6:]:
        copy.wait()
    post.close()


def first(tokens, cotangent, turns, in_rows, out_rows, small, spread, ctx, fsdp):
    rows, width = tokens.shape
    seq = ctx * rows
    own_width = turns.shape[1]
    columns = in_rows.shape[1]
    own_ff = columns - 3 * own_width
    out_total = fsdp * out_rows.shape[0]
    many = 3 * 16 + 3 * 9
    any_, vmem = pl.BlockSpec(memory_space=pl.ANY), pl.BlockSpec(memory_space=pltpu.VMEM)

    def low(*shape):
        return jax.ShapeDtypeStruct(shape, BF16)

    outs = [
        (low(ctx, rows, width), any_), (low(ctx, rows, width), any_), (low(seq, width), any_),
        (jax.ShapeDtypeStruct((seq, 128), F32), vmem),
        (low(seq, own_width), vmem), (low(seq, own_width), vmem), (low(seq, own_width), vmem),
        (low(seq, own_width), vmem), (low(seq, own_ff), vmem), (low(seq, own_ff), vmem),
        (low(fsdp, in_rows.shape[0], columns), any_), (low(out_total, width), vmem),
        (low(ctx, rows, own_width), any_),
        (jax.ShapeDtypeStruct((fsdp,) + small.shape, F32), vmem),
    ]
    chunk_rows = 4 * rows
    return pl.pallas_call(
        first_kernel,
        out_shape=tuple(out[0] for out in outs),
        in_specs=[any_] * 6 + [vmem],
        out_specs=tuple(out[1] for out in outs),
        scratch_shapes=[
            pltpu.VMEM((ctx, rows, width), BF16),
            pltpu.VMEM((ctx, rows, width), BF16),
            pltpu.VMEM((seq, width), BF16),
            pltpu.VMEM((ctx, rows, own_width), BF16),
            pltpu.VMEM((fsdp,) + in_rows.shape, BF16),
            pltpu.VMEM((fsdp,) + out_rows.shape, BF16),
            pltpu.VMEM(out_rows.shape, BF16),
            pltpu.VMEM((fsdp,) + small.shape, BF16),
            pltpu.VMEM((chunk_rows, 3 * own_width), F32),
            pltpu.VMEM((chunk_rows, columns), F32),
            pltpu.VMEM((seq, own_ff), F32),
            pltpu.VMEM((8, width), F32),
            pltpu.VMEM((8, columns), F32),
            pltpu.SemaphoreType.DMA((many,)),
            pltpu.SemaphoreType.DMA((many,)),
            pltpu.SemaphoreType.DMA((12,)),
            pltpu.SemaphoreType.DMA,
            pltpu.SemaphoreType.DMA,
        ],
        compiler_params=pltpu.CompilerParams(
            collective_id=0, has_side_effects=True, vmem_limit_bytes=60 * MIB
        ),
        name="first",
    )(tokens, cotangent, turns, in_rows, out_rows, small, spread)


def attention_kernel(
    block, order, where, q_in, k_in, v_in, g_in, turns, spread, o_out, d_out,
    qs, ks, vs, gs, os, dqs, dks, dvs, score, weight,
):
    rows, width = q_in.shape
    blocks = rows // block

    def collect(at, carry):
        src = pl.ds(pl.multiple_of(where[at] * block, block), block)
        dst = pl.ds(pl.multiple_of(at * block, block), block)
        qs[dst, :] = q_in[src, :]
        ks[dst, :] = k_in[src, :]
        vs[dst, :] = v_in[src, :]
        gs[dst, :] = g_in[src, :]
        return carry

    lax.fori_loop(0, blocks, collect, 0)
    dks[...] = jnp.zeros_like(dks)
    dvs[...] = jnp.zeros_like(dvs)
    heads = width // HEAD_DIM
    scale = HEAD_DIM ** (-0.5)
    q_pos = lax.broadcasted_iota(jnp.int32, (STRIP, STRIP), 0)
    k_pos = lax.broadcasted_iota(jnp.int32, (STRIP, STRIP), 1)
    diagonal = k_pos <= q_pos
    for strip in range(rows // STRIP):
        here = slice(strip * STRIP, (strip + 1) * STRIP)
        for head in range(heads):
            cols = slice(head * HEAD_DIM, (head + 1) * HEAD_DIM)
            query = qs[here, cols] * jnp.asarray(scale, BF16)
            grad = gs[here, cols].astype(F32)
            peak = jnp.full((STRIP, 128), -1e30, F32)
            for chunk in range(strip + 1):
                there = slice(chunk * STRIP, (chunk + 1) * STRIP)
                part = nt_dot(query, ks[there, cols])
                if chunk == strip:
                    part = jnp.where(diagonal, part, -1e30)
                score[chunk] = part
                for lane in range(0, STRIP, 128):
                    peak = jnp.maximum(peak, part[:, lane : lane + 128])
            peak = jnp.max(peak, axis=1, keepdims=True)
            mass = jnp.zeros((STRIP, 128), F32)
            mixed = jnp.zeros((STRIP, HEAD_DIM), F32)
            for chunk in range(strip + 1):
                there = slice(chunk * STRIP, (chunk + 1) * STRIP)
                part = jnp.exp(score[chunk] - peak)
                score[chunk] = part
                for lane in range(0, STRIP, 128):
                    mass = mass + part[:, lane : lane + 128]
                low = part.astype(BF16)
                weight[chunk] = low
                mixed = mixed + dot(low, vs[there, cols])
            inverse = 1.0 / jnp.sum(mass, axis=1, keepdims=True)
            mixed = mixed * inverse
            os[here, cols] = mixed.astype(BF16)
            grad = (grad * inverse).astype(BF16)
            centre = jnp.sum(grad.astype(F32) * mixed, axis=1, keepdims=True)
            d_query = jnp.zeros((STRIP, HEAD_DIM), F32)
            for chunk in range(strip + 1):
                there = slice(chunk * STRIP, (chunk + 1) * STRIP)
                part = nt_dot(grad, vs[there, cols])
                d_score = (score[chunk] * (part - centre)).astype(BF16)
                d_query = d_query + dot(d_score, ks[there, cols])
                dks[there, cols] += tn_dot(d_score, query)
                dvs[there, cols] += tn_dot(weight[chunk], grad)
            dqs[here, cols] = d_query * scale

    def give(at, carry):
        src = pl.ds(pl.multiple_of(order[at] * block, block), block)
        dst = pl.ds(pl.multiple_of(at * block, block), block)
        tables = dot(turns[dst, :], spread[...])
        o_out[dst, :] = os[src, :]
        d_out[dst, :width] = turn(dqs[src, :], tables, True).astype(BF16)
        d_out[dst, width : 2 * width] = turn(dks[src, :], tables, True).astype(BF16)
        d_out[dst, 2 * width :] = dvs[src, :].astype(BF16)
        return carry

    lax.fori_loop(0, blocks, give, 0)


def attention(order, where, block, queries, keys, values, grads, turns, spread):
    rows, width = queries.shape
    vmem = pl.BlockSpec(memory_space=pltpu.VMEM)
    smem = pl.BlockSpec(memory_space=pltpu.SMEM)
    chunks = rows // STRIP
    return pl.pallas_call(
        functools.partial(attention_kernel, block),
        out_shape=(
            jax.ShapeDtypeStruct((rows, width), BF16),
            jax.ShapeDtypeStruct((rows, 3 * width), BF16),
        ),
        in_specs=[smem, smem] + [vmem] * 6,
        out_specs=(vmem, vmem),
        scratch_shapes=[pltpu.VMEM((rows, width), BF16)] * 5
        + [pltpu.VMEM((rows, width), F32)] * 3
        + [pltpu.VMEM((chunks, STRIP, STRIP), F32), pltpu.VMEM((chunks, STRIP, STRIP), BF16)],
        compiler_params=pltpu.CompilerParams(vmem_limit_bytes=48 * MIB),
        cost_estimate=pl.CostEstimate(
            flops=6 * rows * rows * width,
            bytes_accessed=rows * width * 22,
            transcendentals=rows * rows * width // HEAD_DIM // 2,
        ),
        name="attention",
    )(order, where, queries, keys, values, grads, turns, spread)


ORDER = [(2, True), (1, True), (-1, True), (2, False), (0, True), (1, False), (-1, False), (0, False)]
SHARDS = [(2, True), (2, False), (1, True), (-1, True), (1, False), (-1, False), (0, True), (0, False)]


def add_into(target, *parts):
    step = 16

    def body(at, carry):
        take = pl.ds(pl.multiple_of(at * step, step), step)
        total = parts[0][take, :].astype(F32)
        for part in parts[1:]:
            total = total + part[take, :].astype(F32)
        target[take, :] = total.astype(target.dtype)
        return carry

    lax.fori_loop(0, target.shape[0] // step, body, 0)


def reduce_ctx(post, own, core, crossed, pair_in, half_in, ring_in, cross_in, last_in, total):
    place = post.place
    cut = half_in.shape[1]
    up, down, pair = place.to_ctx(1, False), place.to_ctx(-1, False), place.to_ctx(0, True)

    def meet(at, *more):
        crossed[at].wait_recv()
        add_into(core.at[at], own.at[at], core.at[at], *more)

    meet(0)
    far = post.copy(core.at[0], pair_in, pair)
    yield
    meet(1)
    cross_next = post.copy(core.at[1], cross_in.at[0], up)
    meet(2)
    cross_last = post.copy(core.at[2], cross_in.at[1], down)
    yield
    far.wait_recv()
    meet(3, pair_in)
    low = post.copy(core.at[3, pl.ds(0, cut)], half_in.at[0], up)
    high = post.copy(core.at[3, pl.ds(cut, cut)], half_in.at[1], down)
    yield
    cross_next.wait_recv()
    cross_last.wait_recv()
    meet(4, cross_in.at[0], cross_in.at[1])
    last = post.copy(core.at[4], last_in, pair)
    yield
    meet(5)
    low.wait_recv()
    lower = core.at[5, pl.ds(0, cut)]
    add_into(lower, lower, half_in.at[0])
    ring_next = post.copy(core.at[5], ring_in.at[0], up)
    meet(6)
    high.wait_recv()
    upper = core.at[6, pl.ds(cut, cut)]
    add_into(upper, upper, half_in.at[1])
    ring_last = post.copy(core.at[6], ring_in.at[1], down)
    yield
    crossed[7].wait_recv()
    last.wait_recv()
    ring_next.wait_recv()
    ring_last.wait_recv()
    add_into(total, own.at[7], core.at[7], ring_in.at[0], ring_in.at[1], last_in)


def reduce_fsdp(post, part, low_in, high_in, ring_in, pair_in, total):
    place = post.place
    cut, rest = low_in.shape[1], high_in.shape[1]
    lower, upper = pl.ds(0, cut), pl.ds(cut, rest)
    up, down, pair = place.to_fsdp(1, False), place.to_fsdp(-1, False), place.to_fsdp(0, True)
    halves = [
        (
            post.copy(part.at[side, lower], low_in.at[side], up),
            post.copy(part.at[side, upper], high_in.at[side], down),
        )
        for side in range(2)
    ]
    yield
    rings = []
    for side in range(2):
        low, high = halves[side]
        after, before = part.at[2 + 2 * side], part.at[3 + 2 * side]
        low.wait_recv()
        add_into(after.at[lower], after.at[lower], low_in.at[side])
        to_next = post.copy(after, ring_in.at[side, 0], up)
        high.wait_recv()
        add_into(before.at[upper], before.at[upper], high_in.at[side])
        to_last = post.copy(before, ring_in.at[side, 1], down)
        rings.append((to_next, to_last))
        yield
    for copy in rings[0]:
        copy.wait_recv()
    add_into(part.at[6], part.at[6], ring_in.at[0, 0], ring_in.at[0, 1])
    across = post.copy(part.at[6], pair_in, pair)
    yield
    for copy in rings[1]:
        copy.wait_recv()
    across.wait_recv()
    add_into(total, part.at[7], ring_in.at[1, 0], ring_in.at[1, 1], pair_in)


def run(*flows):
    flows = list(flows)
    while flows:
        flows = [flow for flow in flows if next(flow, flows) is not flows]


def second_kernel(
    att, act, d_proj, d_up, w_in, w_out, stat, small, x_own, g_own, x_all, g_all, hidden,
    result, input_grad, in_all, out_all, vector_all,
    own_a, own_b, core_a, core_b, slot_a, slot_b,
    pair_a, half_a, ring_a, cross_a, last_a, pair_b, half_b, ring_b, cross_b, last_b,
    in_part, in_low, in_high, in_ring, in_pair, in_sum,
    out_part, out_low, out_high, out_ring, out_pair, out_sum, out_piece,
    column, x_block, total_a, total_b, vec, gain_sum, shift_sum,
    vector, vector_shards, vector_sum,
    send, recv, local, loads, swap_send, swap_recv,
):
    place = Place()
    post = Post(place, send, recv)
    post.greet()
    rows, width = x_own.shape
    own_width = att.shape[1]
    cut = d_proj.shape[1]
    side = small.shape[2]
    here, shard = place.block(0, False), place.shard(0, False)
    keeps, numbers = [], iter(range(4))

    def keep(source, target):
        copy = pltpu.make_async_copy(source, target, local.at[next(numbers)])
        keeps.append(copy)
        copy.start()
        return copy

    for at in range(small.shape[0]):
        vec[0:4, at * side : (at + 1) * side] = small[at, 0:4, :]
    gain_sum[...] = jnp.zeros_like(gain_sum)
    shift_sum[...] = jnp.zeros_like(shift_sum)

    def load_x(at):
        dy, flip = ORDER[at]
        block = place.block(dy, flip) // 2
        copy = pltpu.make_async_copy(
            x_all.at[pl.ds(2 * block, 2)], x_block.at[at % 2], loads.at[at % 2]
        )
        copy.start()
        return copy

    def load_hidden(at):
        first = pl.multiple_of(place.shard(*SHARDS[at]) * side, side)
        copy = pltpu.make_async_copy(
            hidden.at[:, pl.ds(first, side)], column.at[at % 2], loads.at[2 + at % 2]
        )
        copy.start()
        return copy

    def load_grads(at):
        copy = pltpu.make_async_copy(
            g_all.at[:, pl.ds(at * side, side)], column.at[at % 2], loads.at[4 + at % 2]
        )
        copy.start()
        return copy

    pending_x = [load_x(0)]
    pending_column = [load_hidden(0)]
    crossed_a, crossed_b, slots = {}, {}, {}
    partner = place.to_ctx(0, False, True)
    depth = slot_a.shape[0]

    def produce(at):
        dy, flip = ORDER[at]
        block = place.block(dy, flip) // 2
        pending_x.pop().wait()
        if at + 1 < len(ORDER):
            pending_x.append(load_x(at + 1))
        slot = at % depth
        if at >= depth:
            for copy in slots[at - depth]:
                post.has_left(copy)
        other_rows = pl.ds(pl.multiple_of(block * (2 * rows) + (1 - place.core) * rows, rows), rows)
        own_rows = pl.ds(pl.multiple_of(block * (2 * rows) + place.core * rows, rows), rows)

        def both(ref):
            return jnp.concatenate([ref[other_rows, :], ref[own_rows, :]], axis=0)

        left, right = both(att), both(act)
        span = width // 2
        for first in range(0, width, span):
            take = slice(first, first + span)
            value = dot(left, w_out[:own_width, take]) + dot(right, w_out[own_width:, take])
            slot_a[slot, :, take] = value[:rows].astype(BF16)
            own_a[at, :, take] = value[rows:].astype(BF16)
        left, right, stats = both(d_proj), both(d_up), both(stat)
        mean, inverse = stats[:, 0:1], stats[:, HEAD_DIM : HEAD_DIM + 1]
        span = width // 4
        for first in range(0, width, span):
            take = slice(first, first + span)
            value = nt_dot(left, w_in[take, :cut]) + nt_dot(right, w_in[take, cut:])
            slot_b[slot, :, take] = value[:rows].astype(BF16)
            own_b[at, :, take] = value[rows:].astype(BF16)
            tokens = jnp.concatenate(
                [x_block[at % 2, 1 - place.core, :, take], x_block[at % 2, place.core, :, take]],
                axis=0,
            )
            normed = (tokens.astype(F32) - mean) * inverse
            parts = (2 * rows // 8, 8, span)
            gain_sum[:, take] += jnp.sum((value * normed).reshape(parts), axis=0)
            shift_sum[:, take] += jnp.sum(value.reshape(parts), axis=0)
        crossed_a[at] = post.copy(slot_a.at[slot], core_a.at[at], partner)
        crossed_b[at] = post.copy(slot_b.at[slot], core_b.at[at], partner)
        slots[at] = (crossed_a[at], crossed_b[at])

    def grad_in(at):
        pending_column.pop().wait()
        pending_column.append(load_hidden(at + 1) if at + 1 < len(SHARDS) else load_grads(0))
        rows_of = column[at % 2]
        in_part[at, :, :cut] = tn_dot(rows_of, d_proj[...]).astype(BF16)
        in_part[at, :, cut:] = tn_dot(rows_of, d_up[...]).astype(BF16)

    def grad_out(at):
        pending_column.pop().wait()
        if at + 1 < width // side:
            pending_column.append(load_grads(at + 1))
        columns = column[at % 2]
        take = slice(at * side, (at + 1) * side)
        dense = tn_dot(att[...], columns).astype(BF16)
        fc2 = tn_dot(act[...], columns).astype(BF16)
        dense_step, fc2_step = dense.shape[0] // len(SHARDS), fc2.shape[0] // len(SHARDS)
        for to in range(len(SHARDS)):
            out_part[to, :dense_step, take] = dense[to * dense_step : (to + 1) * dense_step]
            out_part[to, dense_step:, take] = fc2[to * fc2_step : (to + 1) * fc2_step]

    class ByShard:
        @property
        def at(self):
            return self

        def __getitem__(self, index):
            if isinstance(index, tuple):
                return out_part.at[(place.shard(*SHARDS[index[0]]),) + index[1:]]
            return out_part.at[place.shard(*SHARDS[index])]

    def in_flow():
        yield from reduce_fsdp(post, in_part, in_low, in_high, in_ring, in_pair, in_sum)
        keep(in_sum, in_all.at[here])
        yield from gather_ctx(post, in_sum, in_all, in_sum.shape[0] // 2)

    def out_flow():
        yield from reduce_fsdp(post, ByShard(), out_low, out_high, out_ring, out_pair, out_sum)
        swap = Swap(place, out_sum, out_piece, swap_send, swap_recv, local.at[4])
        yield
        swap.wait()
        keep(out_piece, out_all.at[here])
        yield from gather_ctx(post, out_piece, out_all, 48)

    def vector_flow():
        mine = keep(vector, vector_shards.at[shard])
        yield from gather_fsdp(post, vector, vector_shards, 8)
        mine.wait()
        keeps[:] = [kept for kept in keeps if kept is not mine]
        total = vector_shards[0]
        for at in range(1, vector_shards.shape[0]):
            total = total + vector_shards[at]
        vector_sum[...] = total
        keep(vector_sum, vector_all.at[here])
        yield from gather_ctx(post, vector_sum, vector_all, 8)

    ins, outs = in_flow(), out_flow()
    a = reduce_ctx(
        post, own_a, core_a, crossed_a, pair_a, half_a, ring_a, cross_a, last_a, total_a
    )
    b = reduce_ctx(
        post, own_b, core_b, crossed_b, pair_b, half_b, ring_b, cross_b, last_b, total_b
    )
    grad_in(0)
    grad_in(1)
    next(ins)
    produce(0)
    next(a)
    next(b)
    produce(1)
    produce(2)
    next(a)
    next(b)
    grad_in(2)
    grad_in(3)
    produce(3)
    next(ins)
    next(a)
    next(b)
    produce(4)
    grad_in(4)
    grad_in(5)
    next(a)
    next(b)
    next(ins)
    produce(5)
    produce(6)
    next(a)
    next(b)
    grad_in(6)
    grad_in(7)
    next(ins)
    for at in range(width // side):
        grad_out(at)
        if at == 3:
            next(ins)
    next(outs)
    produce(7)

    half = vector.shape[1]
    ones = jnp.ones((16, att.shape[0]), BF16)
    columns = jnp.concatenate([dot(ones, d_proj[...])[:1], dot(ones, d_up[...])[:1]], axis=1)
    vector[...] = jnp.zeros_like(vector)
    sums = [
        jnp.sum(gain_sum[...], axis=0, keepdims=True),
        jnp.sum(shift_sum[...], axis=0, keepdims=True),
        dot(ones[:, :rows], g_own[...])[:1],
    ]
    for at, row in enumerate(sums):
        vector[2 * at : 2 * at + 1, :] = row[:, :half]
        vector[2 * at + 1 : 2 * at + 2, :] = row[:, half:]
    vector[6:7, : columns.shape[1]] = columns
    vectors = vector_flow()
    next(vectors)
    run(ins, outs, a, b, vectors)

    def finish(at, carry):
        step = 16
        take = pl.ds(pl.multiple_of(at * step, step), step)
        stats = stat[pl.ds(pl.multiple_of(here * rows + at * step, step), step), :]
        mean, inverse = stats[:, 0:1], stats[:, HEAD_DIM : HEAD_DIM + 1]
        token = x_own[take, :].astype(F32)
        result[take, :] = (token + total_a[take, :] + vec[2:3, :] + vec[3:4, :]).astype(BF16)
        normed = (token - mean) * inverse
        scaled = total_b[take, :] * vec[0:1, :]
        input_grad[take, :] = g_own[take, :].astype(F32) + inverse * (
            scaled
            - jnp.mean(scaled, axis=1, keepdims=True)
            - normed * jnp.mean(scaled * normed, axis=1, keepdims=True)
        )
        return carry

    lax.fori_loop(0, rows // 16, finish, 0)
    for kept in keeps:
        kept.wait()
    post.close()


def second(att, act, d_proj, d_up, w_in, w_out, stat, small, tokens, cotangent, x_all, g_all, hidden, fsdp):
    rows, width = tokens.shape
    ctx = x_all.shape[0]
    side = width // fsdp
    in_columns, out_rows = w_in.shape[1], w_out.shape[0] // fsdp
    any_, vmem = pl.BlockSpec(memory_space=pl.ANY), pl.BlockSpec(memory_space=pltpu.VMEM)

    def low(*shape):
        return pltpu.VMEM(shape, BF16)

    def wide(*shape):
        return pltpu.VMEM(shape, F32)

    def ctx_slots():
        return [
            low(rows, width), low(2, rows // 2, width), low(2, rows, width), low(2, rows, width),
            low(rows, width),
        ]

    def fsdp_slots(depth, columns, cut):
        return [
            low(fsdp, depth, columns), low(2, cut, columns), low(2, depth - cut, columns),
            low(2, 2, depth, columns), low(depth, columns), low(depth, columns),
        ]

    vector = (16, width // 2)
    many = 2 * 16 + 2 * 9 + 2 * 16 + 9 + 16
    return pl.pallas_call(
        second_kernel,
        out_shape=(
            jax.ShapeDtypeStruct((rows, width), BF16),
            jax.ShapeDtypeStruct((rows, width), F32),
            jax.ShapeDtypeStruct((ctx, side, in_columns), BF16),
            jax.ShapeDtypeStruct((ctx, out_rows, width), BF16),
            jax.ShapeDtypeStruct((ctx,) + vector, F32),
        ),
        in_specs=[vmem] * 10 + [any_] * 3,
        out_specs=(vmem, vmem, any_, any_, any_),
        scratch_shapes=[low(ctx // 2, rows, width)] * 4
        + [low(2, rows, width)] * 2
        + ctx_slots()
        + ctx_slots()
        + fsdp_slots(side, in_columns, side // 2)
        + fsdp_slots(out_rows, width, 48)
        + [low(out_rows, width)]
        + [
            low(2, ctx * rows, side), low(2, 2, rows, width), wide(rows, width), wide(rows, width),
            wide(8, width), wide(8, width), wide(8, width),
            wide(*vector), wide(fsdp, *vector), wide(*vector),
            pltpu.SemaphoreType.DMA((many,)),
            pltpu.SemaphoreType.DMA((many,)),
            pltpu.SemaphoreType.DMA((5,)),
            pltpu.SemaphoreType.DMA((6,)),
            pltpu.SemaphoreType.DMA,
            pltpu.SemaphoreType.DMA,
        ],
        compiler_params=pltpu.CompilerParams(
            collective_id=1, has_side_effects=True, vmem_limit_bytes=63 * MIB
        ),
        name="second",
    )(att, act, d_proj, d_up, w_in, w_out, stat, small, tokens, cotangent, x_all,
      g_all.reshape(ctx * rows, width), hidden)


def widen_kernel(in_all, out_all, qkv, fc1, dense, fc2, in_low, out_low, in_wide, out_wide, loads, stores):
    count = in_all.shape[0]
    fsdp = count // 2
    slots = in_low.shape[0]
    own = qkv.shape[1] // 3 // count
    units = fc1.shape[1] // count
    dense_step, fc2_step = dense.shape[0] // count, fc2.shape[0] // count

    def load(at):
        slot = at % slots
        copies = [
            pltpu.make_async_copy(in_all.at[at], in_low.at[slot], loads.at[slot, 0]),
            pltpu.make_async_copy(out_all.at[at], out_low.at[slot], loads.at[slot, 1]),
        ]
        for copy in copies:
            copy.start()
        return copies

    ahead = [load(at) for at in range(slots - 1)]
    stored = []
    for at in range(count):
        slot = at % slots
        for copy in ahead[at]:
            copy.wait()
        if at + slots - 1 < count:
            ahead.append(load(at + slots - 1))
        if at >= slots:
            for copy in stored[at - slots]:
                copy.wait()
        add_into(in_wide.at[slot], in_low.at[slot])
        add_into(out_wide.at[slot], out_low.at[slot])
        shard, part = at // 2, at % 2
        targets = [
            (in_wide.at[slot, :, pl.ds(0, own)], qkv.at[:, pl.ds(at * own, own)]),
            (in_wide.at[slot, :, pl.ds(own, own)], qkv.at[:, pl.ds((count + at) * own, own)]),
            (in_wide.at[slot, :, pl.ds(2 * own, own)], qkv.at[:, pl.ds((2 * count + at) * own, own)]),
            (in_wide.at[slot, :, pl.ds(3 * own, units)], fc1.at[:, pl.ds(at * units, units)]),
            (
                out_wide.at[slot, pl.ds(0, dense_step)],
                dense.at[pl.ds((part * fsdp + shard) * dense_step, dense_step)],
            ),
            (
                out_wide.at[slot, pl.ds(dense_step, fc2_step)],
                fc2.at[pl.ds((part * fsdp + shard) * fc2_step, fc2_step)],
            ),
        ]
        copies = [
            pltpu.make_async_copy(source, target, stores.at[slot, number])
            for number, (source, target) in enumerate(targets)
        ]
        for copy in copies:
            copy.start()
        stored.append(copies)
    for copies in stored[-slots:]:
        for copy in copies:
            copy.wait()


def widen(in_all, out_all, width, ff, fsdp):
    any_ = pl.BlockSpec(memory_space=pl.ANY)
    slots = 4
    side = width // fsdp
    shapes = [(side, 3 * width), (side, ff), (side, width), (ff // fsdp, width)]
    return pl.pallas_call(
        widen_kernel,
        out_shape=tuple(jax.ShapeDtypeStruct(shape, F32) for shape in shapes),
        in_specs=[any_] * 2,
        out_specs=(any_,) * 4,
        scratch_shapes=[
            pltpu.VMEM((slots,) + in_all.shape[1:], BF16),
            pltpu.VMEM((slots,) + out_all.shape[1:], BF16),
            pltpu.VMEM((slots,) + in_all.shape[1:], F32),
            pltpu.VMEM((slots,) + out_all.shape[1:], F32),
            pltpu.SemaphoreType.DMA((slots, 2)),
            pltpu.SemaphoreType.DMA((slots, 6)),
        ],
        compiler_params=pltpu.CompilerParams(vmem_limit_bytes=32 * MIB),
        name="widen",
    )(in_all, out_all)


def on_device(
    tokens, cotangent, block_order, positions, ln_gain, ln_bias, w_qkv, b_qkv, w_dense, b_dense,
    w_fc1, b_fc1, w_fc2, b_fc2,
):
    ctx, fsdp = lax.axis_size("ctx"), lax.axis_size("fsdp")
    c, f = lax.axis_index("ctx"), lax.axis_index("fsdp")
    share = ctx // fsdp
    rows, width = tokens.shape[1:]
    seq = rows * ctx
    ff = w_fc1.shape[1]
    own_width, own_ff = width // ctx, ff // ctx
    own_rows = width // fsdp
    cut = 3 * own_width
    tokens = tokens.reshape(rows, width)
    cotangent = cotangent.reshape(rows, width)

    vectors = (ln_gain, ln_bias, b_dense, b_fc2, b_qkv, b_fc1)
    small = jnp.concatenate([vector.reshape(-1, own_rows) for vector in vectors])
    small = jnp.pad(small, ((0, 32 - small.shape[0]), (0, 0)))
    in_rows = jnp.concatenate(
        [
            lax.dynamic_slice_in_dim(w_qkv, part * width + c * own_width, own_width, 1)
            for part in range(3)
        ]
        + [lax.dynamic_slice_in_dim(w_fc1, c * own_ff, own_ff, 1)],
        axis=1,
    )

    def own_piece(weight, amount):
        step = amount // fsdp
        return lax.dynamic_slice_in_dim(weight, (c % share) * amount + (c // share) * step, step, 0)

    out_rows = jnp.concatenate([own_piece(w_dense, own_width), own_piece(w_fc2, own_ff)])
    spread = turn_spread(own_width)
    (
        x_all, g_all, hidden, stat, queries, keys, values, d_att, act, d_up, w_in, w_out, turns, small,
    ) = first(
        tokens, cotangent, turn_rows(positions.reshape(rows), own_width), in_rows, out_rows, small,
        spread, ctx, fsdp,
    )
    where = jnp.argsort(block_order).astype(jnp.int32)
    att, d_proj = attention(
        block_order, where, seq // block_order.shape[0], queries, keys, values, d_att,
        turns.reshape(seq, own_width), spread,
    )
    result, input_grad, in_all, out_all, vector = second(
        att, act, d_proj, d_up, w_in.reshape(width, -1), w_out, stat, small, tokens, cotangent, x_all,
        g_all, hidden, fsdp,
    )
    grad_qkv, grad_fc1, grad_dense, grad_fc2 = widen(in_all, out_all, width, ff, fsdp)

    vector = vector.reshape(ctx, -1)
    sums = jnp.sum(vector[:, : 3 * width], axis=0).reshape(3, width)
    sums = lax.dynamic_slice_in_dim(sums, f * own_rows, own_rows, 1)
    columns = vector[:, 3 * width : 3 * width + cut].reshape(ctx, 3, own_width)
    columns = columns.transpose(1, 0, 2).reshape(3 * width)
    units = vector[:, 3 * width + cut : 3 * width + cut + own_ff].reshape(ff)
    return (
        result.reshape(1, rows, width),
        input_grad.reshape(1, rows, width),
        sums[0],
        sums[1],
        grad_qkv,
        lax.dynamic_slice_in_dim(columns, f * (3 * own_rows), 3 * own_rows, 0),
        grad_dense,
        sums[2],
        grad_fc1,
        lax.dynamic_slice_in_dim(units, f * (ff // fsdp), ff // fsdp, 0),
        grad_fc2,
        sums[2],
    )


def solution(mesh):
    split = P("fsdp", "ctx", None)
    matrix = P("fsdp", None)
    vector = P("fsdp")
    return jax.shard_map(
        on_device,
        mesh=mesh,
        in_specs=(split, split, P(), P("fsdp", "ctx"), vector, vector)
        + (matrix, vector) * 4,
        out_specs=(split, split, vector, vector) + (matrix, vector) * 4,
        check_vma=False,
    )
```

time: 1110 us -> 404 us (0.36)
  waiting for transfers between devices: 634 us -> 0 us
  Pallas kernels: 36.6 us -> 365 us
  blocking collectives: 157 us -> 0 us
  matrix products: 114 us -> 0 us
  local copies, waits for them, and re-layouts: 74.7 us -> 26.5 us
  other arithmetic: 43.7 us -> 4.74 us
  starting transfers between devices: 25.4 us -> 0 us
  between operations: 14.9 us -> 1.34 us
    reduce_scatter x6 -> x0, waiting for transfers between devices: 390 us -> none  [the longest x4 199 us: scatter(): lax.psum_scatter(term.astype(BF16), 'fsdp', scatter_dimension=0, tiled=True)]
    pallas_call x0 -> x3, Pallas kernels: none -> 323 us  [the longest x1 182 us: second(): pl.pallas_call(second_kernel, out_shape=(jax.ShapeDtypeStruct((rows, widt...]
    all_gather x7 -> x0, waiting for transfers between devices: 194 us -> none  [the longest x4 115 us: from_ctx(): return lax.all_gather(piece, 'ctx', axis=0)]
    all_gather x3 -> x0, blocking collectives: 157 us -> none  [the longest x1 107 us: on_device(): pos_all = lax.all_gather(positions.reshape(rows), 'ctx', axis=0, tiled=True)]
    dot_general x12 -> x0, matrix products: 114 us -> none  [the longest x1 14.8 us: on_device(): lax.dot_general(d_projected, w_in[:, :cut], NT, preferred_element_type=F32)]
    unnamed x15 -> x0, waiting for transfers between devices: 50 us -> none
    ppermute x3 -> x0, starting transfers between devices: 24.2 us -> none  [the longest x1 21.2 us: on_device(): w_out = lax.ppermute(out_rows, ('ctx', 'fsdp'), swap)]
    reshape x5 -> x7, local copies, waits for them, and re-layouts: 21.7 us -> 4.03 us  [the longest x6 4.02 us: on_device(): vector.reshape(-1, own_rows)]
  transfers between devices with their start and end apart: 17 -> 0, of which waited for: 12 -> 0; matrix products, arithmetic and copies ran while one was open for 19% -> 0% of each run, Pallas kernels for 0% -> 0%
where the time goes in v3:
time: 404 us; the launch traced here: 397 us
  Pallas kernels  365 us (90%)
  local copies, waits for them, and re-layouts  26.5 us (7%)
  other arithmetic  4.74 us (1%)
    pallas_call x1, Pallas kernels, second(): pl.pallas_call(second_kernel, out_shape=(jax.ShapeDtypeStruct((rows, widt...  182 us
    pallas_call x1, Pallas kernels, first(): pl.pallas_call(first_kernel, out_shape=tuple((out[0] for out in outs)), i...  130 us
    pallas_call x1, Pallas kernels, attention(): pl.pallas_call(functools.partial(attention_kernel, block), out_shape=(jax...  41.6 us
    unnamed x36, local copies, waits for them, and re-layouts  15.7 us
    pallas_call x1, Pallas kernels, widen(): pl.pallas_call(widen_kernel, out_shape=tuple((jax.ShapeDtypeStruct(shape,...  11.4 us

profile of v3, /device:TPU:1, one launch (start us, length us, event | category | flops | bytes accessed | tf_op | source)
XLA Modules:
  0.0 397.1 jit_solution(10400184107005627435)
XLA Ops:
  0.6 0.0 copy-start.4
  0.7 1.0 constant_dynamic-slice_fusion.1
  1.7 0.8 constant_dynamic-slice_fusion.2
  2.6 0.7 pad_maximum_fusion.1.out_rows
  3.3 0.9 constant_dynamic-slice_fusion.6
  4.2 1.0 constant_dynamic-slice_fusion.3
  5.2 0.8 pad_maximum_fusion.in_rows
  6.0 0.7 convert_bitcast_fusion
  6.7 0.1 multiply_cosine_fusion
  6.8 0.1 copy.33
  7.0 0.1 copy.32
  7.1 0.1 pad.14.clone
  7.2 0.1 pad.13.clone
  7.3 0.7 maximum_maximum_fusion.turn_in
  8.0 0.7 reshape.97
  8.7 0.7 reshape.98
  9.3 0.7 reshape.93
  10.0 0.7 reshape.94
  10.7 0.7 reshape.95
  11.3 0.7 reshape.96
  12.0 0.1 concatenate.19
  12.1 0.6 pad.4.small_in
  12.7 129.8 %first.1 = (bf16[16,128,2048]{2,1,0:T(8,128)(2,1)}, bf16[16,128,2048]{2,1,0:T(8,128)(2,1)}, bf16[2048,2048]{1,0:T(8,128)(2,1)}, f32[2048,128]{1,0:T(8,128)}, bf1...) custom-call(bf16[128,2048]{1,0:T(8,128)(2,1)} %bitcast.26, ...), custom_call_target="tpu_custom_call" | custom-call | tf_op jit(solution)/shard_map/first/pallas_call | solution.py:461
  142.5 0.0 copy-done.10
  142.5 1.6 sort.17
  144.1 1.0 copy-done.5
  145.2 1.0 copy-done.6
  146.2 1.0 copy-done.7
  147.3 1.0 copy-done.8
  148.3 1.0 copy-done.9
  149.3 41.6 %attention.1 = (bf16[2048,128]{1,0:T(8,128)(2,1)S(1)}, bf16[2048,384]{1,0:T(8,128)(2,1)S(1)}) custom-call(s32[32]{0:T(128)S(1)} %copy-done.10, s32[32]{0:T(128)S(1)} %get-tuple-element.38.where, bf16[2048,128]{1,0:T(8,128)(2,1)S(1)} %copy-done.5, bf16[2048,128]{1,0:T(8,128)(2,1)S(1)} %copy-done.6, bf16[2048,128]{1,0:T(8,128)(2,1)S(1)} %copy-done.7, ...), custom_call_target="tpu_custom_call" | custom-call | flops 3221225472 | bytes 5767168 | tf_op jit(solution)/shard_map/attention/pallas_call | solution.py:577
  190.9 1.1 copy-done.2
  192.0 0.8 copy-done.3
  192.8 181.7 %second.1 = (bf16[128,2048]{1,0:T(8,128)(2,1)}, f32[128,2048]{1,0:T(8,128)}, bf16[16,256,896]{2,1,0:T(8,128)(2,1)}, bf16[16,80,2048]{2,1,0:T(8,128)(2,1)}, f32[16,16,1024]{2,1,0:T(8,128)}) custom-call(bf16[2048,128]{1,0:T(8,128)(2,1)} %copy-done.3, bf16[2048,512]{1,0:T(8,128)(2,1)} %get-tuple-element.45.act, bf16[2048,384]{1,0:T(8,128)(2,1)} %copy-done.2, ...), custom_call_target="tpu_custom_call" | custom-call | tf_op jit(solution)/shard_map/second/pallas_call | solution.py:972
  374.6 0.0 copy-start
  374.6 3.1 copy-done
  377.7 2.5 copy-done.1
  380.2 11.4 %widen.1 = (f32[256,6144]{1,0:T(8,128)}, f32[256,8192]{1,0:T(8,128)}, f32[256,2048]{1,0:T(8,128)}, f32[1024,2048]{1,0:T(8,128)}) custom-call(bf16[16,256,896]{2,1,0:T(8,128)(2,1)S(1)} %copy-done, bf16[16,80,2048]{2,1,0:T(8,128)(2,1)S(1)} %copy-done.1), custom_call_target="tpu_custom_call" | custom-call | tf_op jit(solution)/shard_map/widen/pallas_call | solution.py:1072
  391.6 0.6 copy.35
  392.3 0.7 dynamic_slice.34
  393.0 0.6 dynamic_slice.35
  393.6 0.1 slice_reduce_fusion
  393.7 0.6 fusion.1
  394.3 0.6 copy.40
  394.9 0.8 copy.41
  395.7 0.0 copy-done.11
  395.7 1.0 copy.42
  396.7 0.0 copy-done.14
  (28 shorter events, 0.1 us)
Async XLA Ops:
  0.6 143.5 %copy-start.4 = (bf16[128,384]{1,0:T(8,128)(2,1)S(1)}, bf16[128,384]{1,0:T(8,128)(2,1)}, u32[]{:S(2)}) copy-start(bf16[128,384]{1,0:T(8,128)(2,1)} %constant.76.clone.spread) | copy-start | bytes 294916
  0.7 141.9 %copy-start.10 = (s32[32]{0:T(128)S(1)}, s32[32]{0:T(128)}, u32[]{:S(2)}) copy-start(s32[32]{0:T(128)} %order.1) | copy-start | bytes 388
  144.1 1.0 copy-start.5
  145.2 1.0 copy-start.6
  146.2 1.0 copy-start.7
  147.3 1.0 copy-start.8
  148.3 1.0 copy-start.9
  190.9 1.1 copy-start.2
  192.0 0.8 copy-start.3
  374.6 3.1 copy-start
  377.7 2.5 copy-start.1
  380.2 11.5 %copy-start.12 = (f32[16,16,1024]{2,1,0:T(8,128)S(1)}, f32[16,16,1024]{2,1,0:T(8,128)}, u32[]{:S(2)}) copy-start(f32[16,16,1024]{2,1,0:T(8,128)} %get-tuple-element.57) | copy-start | bytes 3145732
  380.2 14.7 %copy-start.13 = (bf16[128,2048]{1,0:T(8,128)(2,1)S(1)}, bf16[128,2048]{1,0:T(8,128)(2,1)}, u32[]{:S(2)}) copy-start(bf16[128,2048]{1,0:T(8,128)(2,1)} %get-tuple-element.55) | copy-start | bytes 1572868
  391.6 4.1 %copy-start.11 = (f32[128,2048]{1,0:T(8,128)S(1)}, f32[128,2048]{1,0:T(8,128)}, u32[]{:S(2)}) copy-start(f32[128,2048]{1,0:T(8,128)} %get-tuple-element.56) | copy-start | bytes 3145732
  394.3 2.3 copy-start.14
